TPU v7x, 32 devices: a whole 2x2x4 slice. The times are simulated.
32 devices in a mesh: walk: 8 (over z, core), chol: 4 (over y, x).
Axes of the slice: x: 2, y: 2, z: 4, core: 2. Of those that a mesh axis runs over, the one named last changes fastest.
Arguments:
- walkers: float32 [16, 512, 200], P('walk'), as said below
- cholesky: float32 [8, 512, 512], P('chol'), as said below
- fields: float32 [16, 8], P('walk', 'chol'), may hold values from -4 to 4
- weights: float32 [16], P('walk'), may hold values from 0.5 to 2
- counts: int32 [16], P('walk'), may hold values from 0 to 4, as said below
Outputs:
- routed: float32 [16, 512, 200], P('walk')
- comb_marks: float32 [16], P('walk')
Inputs may be any that keep to these rules, and one draw needn't show every extreme that they name: The counts sum to 16. Some walker has 4 copies in every draw. `walkers`: for every walker the intersection matrix (its first 100 rows) differs from the identity by a matrix of spectral norm below one. `cholesky`: each vector is a symmetric matrix.
All inputs are finite; a program needn't handle non-finite values.
Results may differ from a plain program's by a relative error of at most 0.0001.
Values sent between devices are 32-bit elements; how exact they have to be, the bound alone decides.
No kernel may reach another device: no remote copies, remote signals or barrier semaphores. Data moves between devices by JAX's collectives and lax.ppermute only.
A program may use at most 64 MiB of HBM per device.

v0:
```python
import functools
import jax
import jax.numpy as jnp
from jax import lax
from jax.experimental import pallas as pl
from jax.experimental.pallas import tpu as pltpu
from jax.sharding import PartitionSpec as P

TAYLOR = 3
NEWTON = 3
CORES = 2
ROOT_DT = 0.1

f32 = jnp.float32
highest = lax.Precision.HIGHEST
VMEM = pl.BlockSpec(memory_space=pltpu.VMEM)
SMEM = pl.BlockSpec(memory_space=pltpu.SMEM)
PARAMS = pltpu.CompilerParams(vmem_limit_bytes=48 * 2**20)


def dot(left, right, precision=None):
    return jnp.dot(left, right, precision=precision, preferred_element_type=f32)


def ids(rows, columns):
    shape = (rows, columns)
    return (
        lax.broadcasted_iota(jnp.int32, shape, 0),
        lax.broadcasted_iota(jnp.int32, shape, 1),
    )


def up_to(n, unit):
    return -(-n // unit) * unit


def packed(vectors, which):
    m = vectors.shape[1] // 2
    i, j = ids(m, m)
    both = jnp.where(i <= j, vectors[:, :m, :m], vectors[:, m:, m:])
    return jnp.where(which == 0, both, vectors[:, :m, m:])


def prep_kernel(fields, walk, vec, small, other, full, parity):
    count, width, norb = walk.shape
    half = norb // 2
    nelec = width // 2
    pad = up_to(nelec, 128)
    nvec = vec.shape[0]
    i, j = ids(2 * pad, 2 * pad)
    eye = jnp.where((i == j) & (i % pad < nelec), 1.0, 0.0).astype(f32)
    full[...] = jnp.zeros_like(full)
    lane = lax.broadcasted_iota(jnp.int32, (1, small.shape[1]), 1)
    row = jnp.zeros((1, small.shape[1]), f32)
    inside = lax.broadcasted_iota(jnp.int32, (pad, pad), 1) < nelec
    rows = up_to(nelec, 8)
    for w in range(count):
        full[w, :nelec] = walk[w, :nelec]
        full[w, pad : pad + nelec] = walk[w, nelec:]
        over_real = jnp.where(inside, full[w, :pad, :pad], 0.0)
        over_imag = jnp.where(inside, full[w, pad:, :pad], 0.0)
        over = jnp.concatenate(
            [
                jnp.concatenate([over_real, -over_imag], axis=1),
                jnp.concatenate([over_imag, over_real], axis=1),
            ],
            axis=0,
        )
        inv = 2.0 * eye - over
        for _ in range(NEWTON - 1):
            inv = dot(2.0 * eye - dot(inv, over, highest), inv, highest)
        theta = dot(inv, full[w], highest)
        log_part = jnp.zeros((1, 1), f32)
        for g in range(nvec):
            top = vec[g, :rows, :]
            xr = ROOT_DT * jnp.sum(top * theta[:rows], keepdims=True)
            xi = ROOT_DT * jnp.sum(top * theta[pad : pad + rows], keepdims=True)
            field = fields[w, g]
            at = 2 * (w * nvec + g)
            row += jnp.where(lane == at, ROOT_DT * xi, 0.0)
            row += jnp.where(lane == at + 1, ROOT_DT * (field - xr), 0.0)
            log_part += field * xr - 0.5 * (xr * xr - xi * xi)
        row += jnp.where(lane == 2 * count * nvec + w, log_part, 0.0)
    small[...] = jnp.zeros_like(small)
    small[0:1] = row
    i, j = ids(half, half)
    for g in range(nvec):
        corner = vec[g, half:, half:]
        small[g + 1 : g + 2] = jnp.sum(jnp.where(i == j, corner, 0.0), axis=0, keepdims=True)

    @pl.when(parity[0] == 0)
    def _():
        other[...] = vec[:, :half, half:]

    @pl.when(parity[0] != 0)
    def _():
        for g in range(nvec):
            other[g] = jnp.where(i <= j, vec[g, :half, :half], vec[g, half:, half:])


def group_kernel(count, nvec, weights, counts, *refs):
    smalls, out = refs[:-1], refs[-1]
    width = out.shape[1]
    lane = lax.broadcasted_iota(jnp.int32, (1, width), 1)
    per = 2 * count * nvec
    logs = smalls[0][0:1]
    for s in smalls[1:]:
        logs = logs + s[0:1]
    row = jnp.zeros((1, width), f32)
    for k, s in enumerate(smalls):
        mine = jnp.where(lane < per, s[0:1], 0.0)
        row += mine if k == 0 else pltpu.roll(mine, k * per, 1)
    base = per * len(smalls)
    for w in range(count):
        log_weight = jnp.sum(jnp.where(lane == per + w, logs, 0.0), axis=1, keepdims=True)
        row += jnp.where(lane == base + w, weights[w] * jnp.exp(log_weight), 0.0)
        row += jnp.where(lane == base + count + w, counts[w].astype(f32), 0.0)
    out[...] = row


def final_kernel(count, nvec, slots, zs, where_at, *refs):
    refs = list(refs)

    def take(n):
        head = refs[:n]
        del refs[:n]
        return head

    rows = take(zs)
    walks = take(3)
    smalls = take(slots)
    mine = [take(2) for _ in range(slots)]
    theirs = [take(2) for _ in range(slots)]
    out, marks, acc, a_hi, a_lo, source = refs
    me, core = where_at[0], where_at[1]
    z = me // CORES
    per = 2 * count * nvec
    base = per * slots
    width = walks[0].shape[1]
    nelec = width // 2
    norb = walks[0].shape[2]
    half = norb // 2
    part = half // 2
    pad = up_to(nelec, 16)

    total = jnp.float32(0.0)
    before = jnp.float32(0.0)
    base_count = jnp.float32(0.0)
    for k in range(zs):
        for r in range(CORES):
            there = CORES * lax.rem(z - k + zs, zs) + (core if r == 0 else CORES - 1 - core)
            earlier = (there < me).astype(f32)
            for w in range(count):
                weight = rows[k][r, base + w]
                total += weight
                before += earlier * weight
                base_count += earlier * rows[k][r, base + count + w]
    lane = lax.broadcasted_iota(jnp.int32, marks.shape, 1)
    mark_row = jnp.zeros(marks.shape, f32)
    for w in range(count):
        before += rows[0][0, base + w]
        mark_row += jnp.where(lane == w, before, 0.0)
    factor = jnp.full(marks.shape, total, f32)
    marks[...] = (CORES * zs * count) * mark_row / factor

    def behind(at):
        return jnp.where(core == 0, rows[1 % zs][1, at], rows[0][1, at])

    def here(at):
        return rows[0][0, at]

    def ahead(at):
        return jnp.where(core == 0, rows[0][1, at], rows[zs - 1][1, at])

    groups = (behind, here, ahead)
    exists = (
        (me > 0).astype(f32),
        jnp.float32(1.0),
        (me < CORES * zs - 1).astype(f32),
    )
    held = [[groups[q](base + count + w) * exists[q] for w in range(count)] for q in range(3)]
    begin = base_count
    for w in range(count):
        begin -= held[0][w]
    takes = [[] for _ in range(count)]
    for q in range(3):
        for w in range(count):
            end = begin + held[q][w]
            for j in range(count):
                slot = (me * count + j).astype(f32)
                takes[j].append((begin <= slot) & (slot < end))
            begin = end
    coeff = []
    for j in range(count):
        values = []
        for at in range(slots * 2 * nvec):
            slot, rest = divmod(at, 2 * nvec)
            value = jnp.float32(0.0)
            for q in range(3):
                for w in range(count):
                    c = groups[q](slot * per + w * 2 * nvec + rest)
                    value = jnp.where(takes[j][q * count + w], c, value)
            values.append(value)
        coeff.append(values)
        for q in range(3):
            for w in range(count):

                @pl.when(takes[j][q * count + w])
                def _():
                    source[j, :nelec] = walks[q][w, :nelec]
                    source[j, pad : pad + nelec] = walks[q][w, nelec:]

    step = 16
    for side, pieces in enumerate((mine, theirs)):
        at_half = core if side == 0 else CORES - 1 - core
        for p in range(2):

            def add_up(t, _):
                r = pl.multiple_of(t * step, step)
                sums = [jnp.zeros((step, half), f32) for _ in range(2 * count)]
                for k in range(slots):
                    for g in range(nvec):
                        block = pieces[k][p][g, pl.ds(r, step), :]
                        for j in range(count):
                            for ri in range(2):
                                sums[2 * j + ri] += coeff[j][k * 2 * nvec + 2 * g + ri] * block
                for n in range(2 * count):
                    acc[n, at_half, pl.ds(p * part + r, step), :] = sums[n]
                return 0

            lax.fori_loop(0, part // step, add_up, 0)

    i, j_ = ids(half, half)
    for j in range(count):
        for ri in range(2):
            diag = jnp.zeros((1, half), f32)
            for k in range(slots):
                for g in range(nvec):
                    diag += coeff[j][k * 2 * nvec + 2 * g + ri] * smalls[k][g + 1 : g + 2, :]
            square = acc[2 * j + ri, 0]
            turned = square.T
            corner = acc[2 * j + ri, 1]

            def put(value, r, c):
                hi = value.astype(jnp.bfloat16)
                a_hi[j, ri, pl.ds(r, half), pl.ds(c, half)] = hi
                a_lo[j, ri, pl.ds(r, half), pl.ds(c, half)] = (value - hi.astype(f32)).astype(jnp.bfloat16)

            put(jnp.where(i <= j_, square, turned), 0, 0)
            put(jnp.where(i > j_, square, jnp.where(i < j_, turned, diag)), half, half)
            put(corner, 0, half)
            put(corner.T, half, 0)

    for j in range(count):
        for lo in (nelec, pad + nelec):
            source[j, lo : lo + pad - nelec] = jnp.zeros((pad - nelec, norb), f32)
    series = [source[j] for j in range(count)]
    terms = list(series)
    for degree in range(1, TAYLOR + 1):
        for j in range(count):
            term = terms[j]
            hi = term.astype(jnp.bfloat16)
            lo = (term - hi.astype(f32)).astype(jnp.bfloat16)
            both = jnp.concatenate([hi, lo], axis=0)
            prods = []
            for ri in range(2):
                wide = dot(both, a_hi[j, ri])
                prods.append(wide[: 2 * pad] + wide[2 * pad :] + dot(hi, a_lo[j, ri]))
            real = prods[0][:pad] - prods[1][pad:]
            imag = prods[0][pad:] + prods[1][:pad]
            terms[j] = jnp.concatenate([real, imag], axis=0) / degree
            series[j] = series[j] + terms[j]
    for j in range(count):
        out[j, :nelec] = series[j][:nelec]
        out[j, nelec:] = series[j][pad : pad + nelec]


def on_device(walkers, cholesky, fields, weights, counts):
    count, norb, width = walkers.shape
    nvec = cholesky.shape[0]
    half = norb // 2
    part = half // 2
    groups, shards = lax.axis_size("walk"), lax.axis_size("chol")
    zs = groups // CORES
    across = max(d for d in range(1, shards + 1) if shards % d == 0 and d * d <= shards)
    down = shards // across
    me = lax.axis_index("walk").astype(jnp.int32)
    core = me % CORES

    def move(block, dy, dx):
        route = []
        for s in range(shards):
            y, x = divmod(s, across)
            route.append((s, (y + dy) % down * across + (x + dx) % across))
        return lax.ppermute(block, "chol", route)

    def to_core(block):
        return lax.ppermute(block, "walk", [(g, g ^ 1) for g in range(groups)])

    order = [(dy, dx) for dy in range(down) for dx in range(across)]
    own = packed(cholesky, core)
    first, second = own[:, :part], own[:, part:]
    got1, got2 = {(0, 0): first}, {(0, 0): second}
    for dx in range(1, across):
        got1[0, dx] = move(first, 0, dx)
    for dy in range(1, down):
        got2[dy, 0] = move(second, dy, 0)
    for dx in range(1, across):
        got2[0, dx] = move(second, 0, dx)
    for dy in range(1, down):
        got1[dy, 0] = move(first, dy, 0)
    for dy in range(1, down):
        for dx in range(1, across):
            got1[dy, dx] = move(got1[0, dx], dy, 0)
            got2[dy, dx] = move(got2[dy, 0], 0, dx)

    walk_t = jnp.swapaxes(walkers, 1, 2)
    from_behind = lax.ppermute(walk_t, "walk", [(g, g + 1) for g in range(groups - 1)])
    from_ahead = lax.ppermute(walk_t, "walk", [(g + 1, g) for g in range(groups - 1)])

    pad = up_to(width // 2, 128)
    small, other = pl.pallas_call(
        lambda par, fld, wk, vc, sm, ot, fu: prep_kernel(fld, wk, vc, sm, ot, fu, par),
        out_shape=(
            jax.ShapeDtypeStruct((8, half), f32),
            jax.ShapeDtypeStruct((nvec, half, half), f32),
        ),
        in_specs=[SMEM, SMEM, VMEM, VMEM],
        out_specs=(VMEM, VMEM),
        scratch_shapes=[pltpu.VMEM((count, 2 * pad, norb), f32)],
        compiler_params=PARAMS,
        cost_estimate=pl.CostEstimate(flops=5 * 10**9, bytes_accessed=3 * 10**6, transcendentals=0),
    )(core[None], fields, walk_t, cholesky)

    smalls = [small if d == (0, 0) else move(small, *d) for d in order]
    row = pl.pallas_call(
        functools.partial(group_kernel, count, nvec),
        out_shape=jax.ShapeDtypeStruct((1, half), f32),
        in_specs=[SMEM, SMEM] + [VMEM] * shards,
        out_specs=VMEM,
        compiler_params=PARAMS,
    )(weights, counts, *smalls)
    pair = jnp.concatenate([row, to_core(row)], axis=0)
    rows = [pair]
    for k in range(1, zs):
        rows.append(
            lax.ppermute(pair, "walk", [(g, (g + CORES * k) % groups) for g in range(groups)])
        )

    mine = [(got1[d], got2[d]) for d in order]
    theirs = [(other[:, :part], other[:, part:])]
    theirs += [(to_core(got1[d]), to_core(got2[d])) for d in order[1:]]
    flat = [piece for two in mine + theirs for piece in two]
    epad = up_to(width // 2, 16)
    out, marks = pl.pallas_call(
        functools.partial(final_kernel, count, nvec, shards, zs),
        out_shape=(
            jax.ShapeDtypeStruct((count, width, norb), f32),
            jax.ShapeDtypeStruct((1, 128), f32),
        ),
        in_specs=[SMEM] * (1 + zs) + [VMEM] * (3 + shards + len(flat)),
        out_specs=(VMEM, VMEM),
        scratch_shapes=[
            pltpu.VMEM((2 * count, 2, half, half), f32),
            pltpu.VMEM((count, 2, norb, norb), jnp.bfloat16),
            pltpu.VMEM((count, 2, norb, norb), jnp.bfloat16),
            pltpu.VMEM((count, 2 * epad, norb), f32),
        ],
        compiler_params=PARAMS,
        cost_estimate=pl.CostEstimate(flops=10**10, bytes_accessed=10**7, transcendentals=0),
    )(jnp.stack([me, core]), *rows, from_behind, walk_t, from_ahead, *smalls, *flat)
    return jnp.swapaxes(out, 1, 2), marks[0, :count]


def solution(mesh):
    in_specs = (
        P("walk", None, None),
        P("chol", None, None),
        P("walk", "chol"),
        P("walk"),
        P("walk"),
    )
    out_specs = (P("walk", None, None), P("walk"))
    return jax.shard_map(
        on_device, mesh=mesh, in_specs=in_specs, out_specs=out_specs, check_vma=False
    )
```

profile of v0, /device:TPU:0, one launch (start us, length us, event | category | flops | bytes accessed | tf_op | source)
XLA Modules:
  0.0 61.6 jit_solution(241250498093778678)
XLA Ops:
  0.7 1.6 %slice_select_fusion = f32[2,256,256]{2,1,0:T(8,128)S(1)} fusion(f32[2,512,512]{2,1,0:T(8,128)} %vc.1, pred[256,256]{1,0:T(8,128)(4,1)S(1)} %iota_compare_fusion, pred[]{:T(512)S(6)} %eq.5), kind=kLoop, calls=%fused_computation | loop fusion | flops 262144 | bytes 2162689 | tf_op jit(solution)/shard_map/jit(_where)/select_n | solution.py:41
  2.4 3.0 %collective-permute-start.12 = (f32[2,128,256]{2,1,0:T(8,128)S(1)}, f32[2,128,256]{2,1,0:T(8,128)S(1)}, u32[]{:S(2)}, u32[]{:S(2)}) collective-permute-start(f32[2,128,256]{2,1,0:T(8,128)S(1)} %get-tuple-element.12.refs_12_), channel_id=1, source_target_pairs={{0,2},{1,3},{2,0},{3,1},{4,6},{5,7},{6,4},{7,5},{8,10},{9,11},{10,... | collective-permute-start | bytes 786440 | tf_op jit(solution)/shard_map/ppermute | solution.py:295
  5.4 1.5 %collective-permute-start.10 = (f32[2,128,256]{2,1,0:T(8,128)S(1)}, f32[2,128,256]{2,1,0:T(8,128)S(1)}, u32[]{:S(2)}, u32[]{:S(2)}) collective-permute-start(f32[2,128,256]{2,1,0:T(8,128)S(1)} %get-tuple-element.12.refs_12_), channel_id=1, source_target_pairs={{0,1},{1,0},{2,3},{3,2},{4,5},{5,4},{6,7},{7,6},{8,9},{9,8},{10,11... | collective-permute-start | bytes 786440 | tf_op jit(solution)/shard_map/ppermute | solution.py:295
  7.5 5.5 %shard_map.68 = (f32[8,256]{1,0:T(8,128)S(1)}, f32[2,256,256]{2,1,0:T(8,128)S(1)}) custom-call(s32[1]{0:T(128)} %bitcast.1.par, f32[2,2]{1,0:T(2,128)S(1)} %copy-done.4, f32[2,200,512]{2,1,0:T(8,128)S(1)} %bitcast.6, f32[2,512,512]{2,1,0:T(8,128)S(1)} %copy-done), custom_call_target="tpu_custom_call" | custom-call | flops 5000000000 | bytes 3000000 | tf_op jit(solution)/shard_map/pallas_call | solution.py:322
  13.0 1.5 %collective-permute-start.2 = (f32[8,256]{1,0:T(8,128)S(1)}, f32[8,256]{1,0:T(8,128)S(1)}, u32[]{:S(2)}, u32[]{:S(2)}) collective-permute-start(f32[8,256]{1,0:T(8,128)S(1)} %get-tuple-element.6.refs_0_.refs_7_), channel_id=1, source_target_pairs={{0,3},{1,2},{2,1},{3,0},{4,7},{5,6},{6,5},{7,4},{8,11},{9,10},{10,... | collective-permute-start | bytes 24584 | tf_op jit(solution)/shard_map/ppermute | solution.py:295
  14.6 3.0 %collective-permute-done.2.refs_3_.refs_10_ = f32[8,256]{1,0:T(8,128)S(1)} collective-permute-done((f32[8,256]{1,0:T(8,128)S(1)}, f32[8,256]{1,0:T(8,128)S(1)}, u32[]{:S(2)}, u32[]{:S(2)}) %collective-permute-start.2) | collective-permute-done | bytes 8224 | tf_op jit(solution)/shard_map/ppermute | solution.py:295
  18.2 3.1 %collective-permute-done.refs_1_.refs_8_ = f32[8,256]{1,0:T(8,128)S(1)} collective-permute-done((f32[8,256]{1,0:T(8,128)S(1)}, f32[8,256]{1,0:T(8,128)S(1)}, u32[]{:S(2)}, u32[]{:S(2)}) %collective-permute-start) | collective-permute-done | bytes 8224 | tf_op jit(solution)/shard_map/ppermute | solution.py:295
  21.3 0.6 %shard_map.69 = f32[1,256]{1,0:T(1,128)S(1)} custom-call(f32[2]{0:T(128)S(1)} %copy-done.1, s32[2]{0:T(128)S(1)} %copy-done.2, f32[8,256]{1,0:T(8,128)S(1)} %get-tuple-element.6.refs_0_.refs_7_, f32[8,256]{1,0:T(8,128)S(1)} %collective-permute-done.refs_1_.refs_8_, f32[8,256]{1,0:T(8,128)S(1)} %collective-permute-done.1.refs_2_.refs_9_, ...), custom_call_target="tpu_custom_call" | custom-call | tf_op jit(solution)/shard_map/pallas_call | solution.py:336
  22.0 1.1 %collective-permute-done.3 = f32[1,256]{1,0:T(1,128)S(1)} collective-permute-done((f32[1,256]{1,0:T(1,128)S(1)}, f32[1,256]{1,0:T(1,128)S(1)}, u32[]{:S(2)}, u32[]{:S(2)}) %collective-permute-start.3) | collective-permute-done | bytes 1056 | tf_op jit(solution)/shard_map/ppermute | solution.py:298
  23.1 3.7 %collective-permute-start.6 = (f32[2,256]{1,0:T(2,128)S(1)}, f32[2,256]{1,0:T(2,128)S(1)}, u32[]{:S(2)}, u32[]{:S(2)}) collective-permute-start(f32[2,256]{1,0:T(2,128)S(1)} %pad_maximum_fusion.refs_0_), channel_id=1, source_target_pairs={{0,24},{4,28},{8,0},{12,4},{16,8},{20,12},{24,16},{28,20},{1,25},{... | collective-permute-start | bytes 6152 | tf_op jit(solution)/shard_map/ppermute | solution.py:347
  26.8 1.3 %collective-permute-done.6.refs_3_ = f32[2,256]{1,0:T(2,128)S(1)} collective-permute-done((f32[2,256]{1,0:T(2,128)S(1)}, f32[2,256]{1,0:T(2,128)S(1)}, u32[]{:S(2)}, u32[]{:S(2)}) %collective-permute-start.6) | collective-permute-done | bytes 2080 | tf_op jit(solution)/shard_map/ppermute | solution.py:347
  28.4 2.9 %collective-permute-done.5.refs_2_ = f32[2,256]{1,0:T(2,128)S(1)} collective-permute-done((f32[2,256]{1,0:T(2,128)S(1)}, f32[2,256]{1,0:T(2,128)S(1)}, u32[]{:S(2)}, u32[]{:S(2)}) %collective-permute-start.5) | collective-permute-done | bytes 2080 | tf_op jit(solution)/shard_map/ppermute | solution.py:347
  31.3 0.5 collective-permute-start.9
  31.8 1.9 %collective-permute-done.4.refs_1_ = f32[2,256]{1,0:T(2,128)S(1)} collective-permute-done((f32[2,256]{1,0:T(2,128)S(1)}, f32[2,256]{1,0:T(2,128)S(1)}, u32[]{:S(2)}, u32[]{:S(2)}) %collective-permute-start.4) | collective-permute-done | bytes 2080 | tf_op jit(solution)/shard_map/ppermute | solution.py:347
  33.7 0.5 collective-permute-start.14
  34.3 1.3 %collective-permute-start.8 = (f32[2,200,512]{2,1,0:T(8,128)S(1)}, f32[2,200,512]{2,1,0:T(8,128)S(1)}, u32[]{:S(2)}, u32[]{:S(2)}) collective-permute-start(f32[2,200,512]{2,1,0:T(8,128)S(1)} %bitcast.7), channel_id=1, source_target_pairs={{4,0},{8,4},{12,8},{16,12},{20,16},{24,20},{28,24},{5,1},{9,5},{13... | collective-permute-start | bytes 2457608 | tf_op jit(solution)/shard_map/ppermute | solution.py:319
  35.6 3.1 %collective-permute-start.7 = (f32[2,200,512]{2,1,0:T(8,128)S(1)}, f32[2,200,512]{2,1,0:T(8,128)S(1)}, u32[]{:S(2)}, u32[]{:S(2)}) collective-permute-start(f32[2,200,512]{2,1,0:T(8,128)S(1)} %bitcast.8), channel_id=1, source_target_pairs={{0,4},{4,8},{8,12},{12,16},{16,20},{20,24},{24,28},{1,5},{5,9},{9,... | collective-permute-start | bytes 2457608 | tf_op jit(solution)/shard_map/ppermute | solution.py:318
  38.7 1.9 %collective-permute-done.9.refs_13_ = f32[2,128,256]{2,1,0:T(8,128)S(1)} collective-permute-done((f32[2,128,256]{2,1,0:T(8,128)S(1)}, f32[2,128,256]{2,1,0:T(8,128)S(1)}, u32[]{:S(2)}, u32[]{:S(2)}) %collective-permute-start.9) | collective-permute-done | bytes 262176 | tf_op jit(solution)/shard_map/ppermute | solution.py:295
  41.0 2.8 %collective-permute-done.14.refs_18_ = f32[2,128,256]{2,1,0:T(8,128)S(1)} collective-permute-done((f32[2,128,256]{2,1,0:T(8,128)S(1)}, f32[2,128,256]{2,1,0:T(8,128)S(1)}, u32[]{:S(2)}, u32[]{:S(2)}) %collective-permute-start.14) | collective-permute-done | bytes 262176 | tf_op jit(solution)/shard_map/ppermute | solution.py:295
  43.9 1.5 %collective-permute-start.13 = (f32[2,128,256]{2,1,0:T(8,128)S(1)}, f32[2,128,256]{2,1,0:T(8,128)S(1)}, u32[]{:S(2)}, u32[]{:S(2)}) collective-permute-start(f32[2,128,256]{2,1,0:T(8,128)S(1)} %collective-permute-done.9.refs_13_), channel_id=1, source_target_pairs={{0,2},{1,3},{2,0},{3,1},{4,6},{5,7},{6,4},{7,5},{8,10},{9,11},{10,... | collective-permute-start | bytes 786440 | tf_op jit(solution)/shard_map/ppermute | solution.py:295
  45.9 4.3 %collective-permute-done.13.refs_17_ = f32[2,128,256]{2,1,0:T(8,128)S(1)} collective-permute-done((f32[2,128,256]{2,1,0:T(8,128)S(1)}, f32[2,128,256]{2,1,0:T(8,128)S(1)}, u32[]{:S(2)}, u32[]{:S(2)}) %collective-permute-start.13) | collective-permute-done | bytes 262176 | tf_op jit(solution)/shard_map/ppermute | solution.py:295
  50.4 1.4 %collective-permute-done.19.refs_25_ = f32[2,128,256]{2,1,0:T(8,128)S(1)} collective-permute-done((f32[2,128,256]{2,1,0:T(8,128)S(1)}, f32[2,128,256]{2,1,0:T(8,128)S(1)}, u32[]{:S(2)}, u32[]{:S(2)}) %collective-permute-start.19) | collective-permute-done | bytes 262176 | tf_op jit(solution)/shard_map/ppermute | solution.py:298
  51.8 0.9 %copy-done.5 = f32[2,200,512]{2,1,0:T(8,128)} copy-done((f32[2,200,512]{2,1,0:T(8,128)}, f32[2,200,512]{2,1,0:T(8,128)S(1)}, u32[]{:S(2)}) %copy-start.5) | copy-done | bytes 819224
  52.7 8.4 %shard_map.70 = (f32[2,200,512]{2,1,0:T(8,128)}, f32[1,128]{1,0:T(1,128)S(1)}) custom-call(s32[2]{0:T(128)S(1)} %pad_add_fusion.where_at, f32[2,256]{1,0:T(2,128)S(1)} %pad_maximum_fusion.refs_0_, f32[2,256]{1,0:T(2,128)S(1)} %collective-permute-done.4.refs_1_, f32[2,256]{1,0:T(2,128)S(1)} %collective-permute-done.5.refs_2_, ...), custom_call_target="tpu_custom_call" | custom-call | flops 10000000000 | bytes 10000000 | tf_op jit(solution)/shard_map/pallas_call | solution.py:355
  (40 shorter events, 3.3 us)
Async XLA Ops:
  0.6 6.8 %copy-start = (f32[2,512,512]{2,1,0:T(8,128)S(1)}, f32[2,512,512]{2,1,0:T(8,128)}, u32[]{:S(2)}) copy-start(f32[2,512,512]{2,1,0:T(8,128)} %vc.1) | copy-start | bytes 6291460
  2.4 29.4 %collective-permute-start.12 = (f32[2,128,256]{2,1,0:T(8,128)S(1)}, f32[2,128,256]{2,1,0:T(8,128)S(1)}, u32[]{:S(2)}, u32[]{:S(2)}) collective-permute-start(f32[2,128,256]{2,1,0:T(8,128)S(1)} %get-tuple-element.12.refs_12_), channel_id=1, source_target_pairs={{0,2},{1,3},{2,0},{3,1},{4,6},{5,7},{6,4},{7,5},{8,10},{9,11},{10,... | collective-permute-start | bytes 786440 | tf_op jit(solution)/shard_map/ppermute | solution.py:295
  5.4 28.8 %collective-permute-start.10 = (f32[2,128,256]{2,1,0:T(8,128)S(1)}, f32[2,128,256]{2,1,0:T(8,128)S(1)}, u32[]{:S(2)}, u32[]{:S(2)}) collective-permute-start(f32[2,128,256]{2,1,0:T(8,128)S(1)} %get-tuple-element.12.refs_12_), channel_id=1, source_target_pairs={{0,1},{1,0},{2,3},{3,2},{4,5},{5,4},{6,7},{7,6},{8,9},{9,8},{10,11... | collective-permute-start | bytes 786440 | tf_op jit(solution)/shard_map/ppermute | solution.py:295
  6.9 28.6 %collective-permute-start.11 = (f32[2,128,256]{2,1,0:T(8,128)S(1)}, f32[2,128,256]{2,1,0:T(8,128)S(1)}, u32[]{:S(2)}, u32[]{:S(2)}) collective-permute-start(f32[2,128,256]{2,1,0:T(8,128)S(1)} %get-tuple-element.13.refs_11_), channel_id=1, source_target_pairs={{0,2},{1,3},{2,0},{3,1},{4,6},{5,7},{6,4},{7,5},{8,10},{9,11},{10,... | collective-permute-start | bytes 786440 | tf_op jit(solution)/shard_map/ppermute | solution.py:295
  7.4 13.8 %copy-start.1 = (f32[2]{0:T(128)S(1)}, f32[2]{0:T(128)}, u32[]{:S(2)}) copy-start(f32[2]{0:T(128)} %weights.1) | copy-start | bytes 28
  7.5 13.8 %copy-start.2 = (s32[2]{0:T(128)S(1)}, s32[2]{0:T(128)}, u32[]{:S(2)}) copy-start(s32[2]{0:T(128)} %counts.1) | copy-start | bytes 28
  13.0 4.7 %collective-permute-start.2 = (f32[8,256]{1,0:T(8,128)S(1)}, f32[8,256]{1,0:T(8,128)S(1)}, u32[]{:S(2)}, u32[]{:S(2)}) collective-permute-start(f32[8,256]{1,0:T(8,128)S(1)} %get-tuple-element.6.refs_0_.refs_7_), channel_id=1, source_target_pairs={{0,3},{1,2},{2,1},{3,0},{4,7},{5,6},{6,5},{7,4},{8,11},{9,10},{10,... | collective-permute-start | bytes 24584 | tf_op jit(solution)/shard_map/ppermute | solution.py:295
  14.5 3.7 %collective-permute-start.1 = (f32[8,256]{1,0:T(8,128)S(1)}, f32[8,256]{1,0:T(8,128)S(1)}, u32[]{:S(2)}, u32[]{:S(2)}) collective-permute-start(f32[8,256]{1,0:T(8,128)S(1)} %get-tuple-element.6.refs_0_.refs_7_), channel_id=1, source_target_pairs={{0,2},{1,3},{2,0},{3,1},{4,6},{5,7},{6,4},{7,5},{8,10},{9,11},{10,... | collective-permute-start | bytes 24584 | tf_op jit(solution)/shard_map/ppermute | solution.py:295
  17.6 3.7 %collective-permute-start = (f32[8,256]{1,0:T(8,128)S(1)}, f32[8,256]{1,0:T(8,128)S(1)}, u32[]{:S(2)}, u32[]{:S(2)}) collective-permute-start(f32[8,256]{1,0:T(8,128)S(1)} %get-tuple-element.6.refs_0_.refs_7_), channel_id=1, source_target_pairs={{0,1},{1,0},{2,3},{3,2},{4,5},{5,4},{6,7},{7,6},{8,9},{9,8},{10,11... | collective-permute-start | bytes 24584 | tf_op jit(solution)/shard_map/ppermute | solution.py:295
  21.9 1.2 %collective-permute-start.3 = (f32[1,256]{1,0:T(1,128)S(1)}, f32[1,256]{1,0:T(1,128)S(1)}, u32[]{:S(2)}, u32[]{:S(2)}) collective-permute-start(f32[1,256]{1,0:T(1,128)S(1)} %shard_map.69), channel_id=1, source_target_pairs={{0,4},{4,0},{8,12},{12,8},{16,20},{20,16},{24,28},{28,24},{1,5},{5... | collective-permute-start | bytes 3080 | tf_op jit(solution)/shard_map/ppermute | solution.py:298
  23.1 5.0 %collective-permute-start.6 = (f32[2,256]{1,0:T(2,128)S(1)}, f32[2,256]{1,0:T(2,128)S(1)}, u32[]{:S(2)}, u32[]{:S(2)}) collective-permute-start(f32[2,256]{1,0:T(2,128)S(1)} %pad_maximum_fusion.refs_0_), channel_id=1, source_target_pairs={{0,24},{4,28},{8,0},{12,4},{16,8},{20,12},{24,16},{28,20},{1,25},{... | collective-permute-start | bytes 6152 | tf_op jit(solution)/shard_map/ppermute | solution.py:347
  26.8 4.5 %collective-permute-start.5 = (f32[2,256]{1,0:T(2,128)S(1)}, f32[2,256]{1,0:T(2,128)S(1)}, u32[]{:S(2)}, u32[]{:S(2)}) collective-permute-start(f32[2,256]{1,0:T(2,128)S(1)} %pad_maximum_fusion.refs_0_), channel_id=1, source_target_pairs={{0,16},{4,20},{8,24},{12,28},{16,0},{20,4},{24,8},{28,12},{1,17},{... | collective-permute-start | bytes 6152 | tf_op jit(solution)/shard_map/ppermute | solution.py:347
  28.1 5.6 %collective-permute-start.4 = (f32[2,256]{1,0:T(2,128)S(1)}, f32[2,256]{1,0:T(2,128)S(1)}, u32[]{:S(2)}, u32[]{:S(2)}) collective-permute-start(f32[2,256]{1,0:T(2,128)S(1)} %pad_maximum_fusion.refs_0_), channel_id=1, source_target_pairs={{0,8},{4,12},{8,16},{12,20},{16,24},{20,28},{24,0},{28,4},{1,9},{5... | collective-permute-start | bytes 6152 | tf_op jit(solution)/shard_map/ppermute | solution.py:347
  31.3 9.2 %collective-permute-start.9 = (f32[2,128,256]{2,1,0:T(8,128)S(1)}, f32[2,128,256]{2,1,0:T(8,128)S(1)}, u32[]{:S(2)}, u32[]{:S(2)}) collective-permute-start(f32[2,128,256]{2,1,0:T(8,128)S(1)} %get-tuple-element.13.refs_11_), channel_id=1, source_target_pairs={{0,1},{1,0},{2,3},{3,2},{4,5},{5,4},{6,7},{7,6},{8,9},{9,8},{10,11... | collective-permute-start | bytes 786440 | tf_op jit(solution)/shard_map/ppermute | solution.py:295
  31.8 8.7 %collective-permute-start.18 = (f32[2,128,256]{2,1,0:T(8,128)S(1)}, f32[2,128,256]{2,1,0:T(8,128)S(1)}, u32[]{:S(2)}, u32[]{:S(2)}) collective-permute-start(f32[2,128,256]{2,1,0:T(8,128)S(1)} %collective-permute-done.12.refs_16_), channel_id=1, source_target_pairs={{0,4},{4,0},{8,12},{12,8},{16,20},{20,16},{24,28},{28,24},{1,5},{5... | collective-permute-start | bytes 786440 | tf_op jit(solution)/shard_map/ppermute | solution.py:298
  33.7 10.1 %collective-permute-start.14 = (f32[2,128,256]{2,1,0:T(8,128)S(1)}, f32[2,128,256]{2,1,0:T(8,128)S(1)}, u32[]{:S(2)}, u32[]{:S(2)}) collective-permute-start(f32[2,128,256]{2,1,0:T(8,128)S(1)} %collective-permute-done.12.refs_16_), channel_id=1, source_target_pairs={{0,1},{1,0},{2,3},{3,2},{4,5},{5,4},{6,7},{7,6},{8,9},{9,8},{10,11... | collective-permute-start | bytes 786440 | tf_op jit(solution)/shard_map/ppermute | solution.py:295
  34.3 17.5 %collective-permute-start.8 = (f32[2,200,512]{2,1,0:T(8,128)S(1)}, f32[2,200,512]{2,1,0:T(8,128)S(1)}, u32[]{:S(2)}, u32[]{:S(2)}) collective-permute-start(f32[2,200,512]{2,1,0:T(8,128)S(1)} %bitcast.7), channel_id=1, source_target_pairs={{4,0},{8,4},{12,8},{16,12},{20,16},{24,20},{28,24},{5,1},{9,5},{13... | collective-permute-start | bytes 2457608 | tf_op jit(solution)/shard_map/ppermute | solution.py:319
  35.6 16.2 %collective-permute-start.7 = (f32[2,200,512]{2,1,0:T(8,128)S(1)}, f32[2,200,512]{2,1,0:T(8,128)S(1)}, u32[]{:S(2)}, u32[]{:S(2)}) collective-permute-start(f32[2,200,512]{2,1,0:T(8,128)S(1)} %bitcast.8), channel_id=1, source_target_pairs={{0,4},{4,8},{8,12},{12,16},{16,20},{20,24},{24,28},{1,5},{5,9},{9,... | collective-permute-start | bytes 2457608 | tf_op jit(solution)/shard_map/ppermute | solution.py:318
  40.5 4.9 %collective-permute-start.16 = (f32[2,128,256]{2,1,0:T(8,128)S(1)}, f32[2,128,256]{2,1,0:T(8,128)S(1)}, u32[]{:S(2)}, u32[]{:S(2)}) collective-permute-start(f32[2,128,256]{2,1,0:T(8,128)S(1)} %collective-permute-done.10.refs_14_), channel_id=1, source_target_pairs={{0,4},{4,0},{8,12},{12,8},{16,20},{20,16},{24,28},{28,24},{1,5},{5... | collective-permute-start | bytes 786440 | tf_op jit(solution)/shard_map/ppermute | solution.py:298
  40.5 4.9 %collective-permute-start.17 = (f32[2,128,256]{2,1,0:T(8,128)S(1)}, f32[2,128,256]{2,1,0:T(8,128)S(1)}, u32[]{:S(2)}, u32[]{:S(2)}) collective-permute-start(f32[2,128,256]{2,1,0:T(8,128)S(1)} %collective-permute-done.11.refs_15_), channel_id=1, source_target_pairs={{0,4},{4,0},{8,12},{12,8},{16,20},{20,16},{24,28},{28,24},{1,5},{5... | collective-permute-start | bytes 786440 | tf_op jit(solution)/shard_map/ppermute | solution.py:298
  43.9 6.4 %collective-permute-start.13 = (f32[2,128,256]{2,1,0:T(8,128)S(1)}, f32[2,128,256]{2,1,0:T(8,128)S(1)}, u32[]{:S(2)}, u32[]{:S(2)}) collective-permute-start(f32[2,128,256]{2,1,0:T(8,128)S(1)} %collective-permute-done.9.refs_13_), channel_id=1, source_target_pairs={{0,2},{1,3},{2,0},{3,1},{4,6},{5,7},{6,4},{7,5},{8,10},{9,11},{10,... | collective-permute-start | bytes 786440 | tf_op jit(solution)/shard_map/ppermute | solution.py:295
  45.4 5.0 %collective-permute-start.15 = (f32[2,128,256]{2,1,0:T(8,128)S(1)}, f32[2,128,256]{2,1,0:T(8,128)S(1)}, u32[]{:S(2)}, u32[]{:S(2)}) collective-permute-start(f32[2,128,256]{2,1,0:T(8,128)S(1)} %collective-permute-done.9.refs_13_), channel_id=1, source_target_pairs={{0,4},{4,0},{8,12},{12,8},{16,20},{20,16},{24,28},{28,24},{1,5},{5... | collective-permute-start | bytes 786440 | tf_op jit(solution)/shard_map/ppermute | solution.py:298
  45.4 5.0 %collective-permute-start.20 = (f32[2,128,256]{2,1,0:T(8,128)S(1)}, f32[2,128,256]{2,1,0:T(8,128)S(1)}, u32[]{:S(2)}, u32[]{:S(2)}) collective-permute-start(f32[2,128,256]{2,1,0:T(8,128)S(1)} %collective-permute-done.14.refs_18_), channel_id=1, source_target_pairs={{0,4},{4,0},{8,12},{12,8},{16,20},{20,16},{24,28},{28,24},{1,5},{5... | collective-permute-start | bytes 786440 | tf_op jit(solution)/shard_map/ppermute | solution.py:298
  50.2 1.5 %collective-permute-start.19 = (f32[2,128,256]{2,1,0:T(8,128)S(1)}, f32[2,128,256]{2,1,0:T(8,128)S(1)}, u32[]{:S(2)}, u32[]{:S(2)}) collective-permute-start(f32[2,128,256]{2,1,0:T(8,128)S(1)} %collective-permute-done.13.refs_17_), channel_id=1, source_target_pairs={{0,4},{4,0},{8,12},{12,8},{16,20},{20,16},{24,28},{28,24},{1,5},{5... | collective-permute-start | bytes 786440 | tf_op jit(solution)/shard_map/ppermute | solution.py:298
  (3 other events, 14.5 us)
where the time goes:
time: 61.8 us; the launch traced here: 61.6 us
  waiting for transfers between devices  24.2 us (39%)
  starting transfers between devices  18.8 us (30%)
  Pallas kernels  14.5 us (23%)
  other arithmetic  1.75 us (3%)
  local copies, waits for them, and re-layouts  1.51 us (2%)
  between operations  0.8 us (1%)
    ppermute x9, waiting for transfers between devices, move(): return lax.ppermute(block, 'chol', route)  15.5 us
    ppermute x9, starting transfers between devices, move(): return lax.ppermute(block, 'chol', route)  9.43 us
    pallas_call x1, Pallas kernels, on_device(): pl.pallas_call(functools.partial(final_kernel, count, nvec, shards, zs),...  8.37 us
    ppermute x3, waiting for transfers between devices, on_device(): lax.ppermute(pair, 'walk', [(g, (g + CORES * k) % groups) for g in range(...  6.16 us
    pallas_call x1, Pallas kernels, on_device(): pl.pallas_call(lambda par, fld, wk, vc, sm, ot, fu: prep_kernel(fld, wk,...  5.5 us
    ppermute x3, starting transfers between devices, on_device(): lax.ppermute(pair, 'walk', [(g, (g + CORES * k) % groups) for g in range(...  3.91 us
    ppermute x1, starting transfers between devices, on_device(): lax.ppermute(walk_t, 'walk', [(g, g + 1) for g in range(groups - 1)])  3.08 us
    ppermute x7, waiting for transfers between devices, to_core(): return lax.ppermute(block, 'walk', [(g, g ^ 1) for g in range(groups)])  2.54 us
  transfers between devices with their start and end apart: 21, of which 11 were waited for; matrix products, arithmetic and copies ran while one was open for 0% of the time, Pallas kernels for 10%

commit v1 on v0

v1 whole, which is shorter than its diff:
```python
import functools
import jax
import jax.numpy as jnp
from jax import lax
from jax.experimental import pallas as pl
from jax.experimental.pallas import tpu as pltpu
from jax.sharding import PartitionSpec as P

TAYLOR = 3
NEWTON = 3
CORES = 2
ROOT_DT = 0.1
SMALL = 8
EARLY_COST = 0
K_COST = 0
K2_COST = 4 * 10**9
EDGE_STEP = 0
LATE_COST = 10 * 10**9

f32 = jnp.float32
highest = lax.Precision.HIGHEST
VMEM = pl.BlockSpec(memory_space=pltpu.VMEM)
SMEM = pl.BlockSpec(memory_space=pltpu.SMEM)
HBM = pl.BlockSpec(memory_space=pltpu.HBM)
PARAMS = pltpu.CompilerParams(vmem_limit_bytes=24 * 2**20)


def dot(left, right, precision=None):
    return jnp.dot(left, right, precision=precision, preferred_element_type=f32)


def ids(rows, columns):
    shape = (rows, columns)
    return (
        lax.broadcasted_iota(jnp.int32, shape, 0),
        lax.broadcasted_iota(jnp.int32, shape, 1),
    )


def up_to(n, unit):
    return -(-n // unit) * unit


def pack_kernel(which, vec, first, second, other, top, diags):
    nvec, norb = vec.shape[:2]
    half = norb // 2
    part = half // 2
    rows = top.shape[1]
    i, j = ids(part, half)

    def write(triangles, corners):
        for g in range(nvec):
            for n in range(2):
                rows_in = pl.ds(n * part, part)
                rows_out = pl.ds(g * part, part)
                lower = vec[g, pl.ds(half + n * part, part), half:]
                triangles[n][rows_out] = jnp.where(i + n * part <= j, vec[g, rows_in, :half], lower)
                corners[n][rows_out] = vec[g, rows_in, half:]

    @pl.when(which[1] == 0)
    def _():
        write((first, second), (other.at[0], other.at[1]))

    @pl.when(which[1] != 0)
    def _():
        write((other.at[0], other.at[1]), (first, second))

    diags[...] = jnp.zeros_like(diags)
    i, j = ids(half, half)
    for g in range(nvec):
        top[g] = vec[g, :rows]
        corner = jnp.where(i == j, vec[g, half:, half:], 0.0)
        diags[g + 1 : g + 2] = jnp.sum(corner, axis=0, keepdims=True)


def pack(which, cholesky, rows):
    nvec, norb = cholesky.shape[:2]
    half = norb // 2
    piece = (nvec * half // 2, half)
    return pl.pallas_call(
        pack_kernel,
        out_shape=tuple(
            jax.ShapeDtypeStruct(shape, f32)
            for shape in (piece, piece, (2, *piece), (nvec, rows, norb), (SMALL, half))
        ),
        in_specs=[SMEM, VMEM],
        out_specs=(VMEM,) * 5,
        compiler_params=PARAMS,
        cost_estimate=pl.CostEstimate(flops=10**6, bytes_accessed=4 * 10**6, transcendentals=0),
    )(which, cholesky)


def prep_kernel(fields, walk, tops, diags, small, full):
    count, width, norb = walk.shape
    half = norb // 2
    nelec = width // 2
    pad = up_to(nelec, 128)
    nvec = tops.shape[0]
    i, j = ids(pad, pad)
    twice = jnp.concatenate(
        [jnp.where((i == j) & (i < nelec), 2.0, 0.0), jnp.zeros((pad, pad))], axis=1
    ).astype(f32)
    inside = j < nelec
    full[...] = jnp.zeros_like(full)

    def spread(top):
        return jnp.concatenate(
            [top, jnp.concatenate([-top[:, pad:], top[:, :pad]], axis=1)], axis=0
        )

    inv, over = [], []
    for w in range(count):
        full[w, :nelec] = walk[w, :nelec]
        full[w, pad : pad + nelec] = walk[w, nelec:]
        over_real = jnp.where(inside, full[w, :pad, :pad], 0.0)
        over_imag = jnp.where(inside, full[w, pad:, :pad], 0.0)
        top = jnp.concatenate([over_real, -over_imag], axis=1)
        inv.append(twice - top)
        over.append(spread(top))
    for _ in range(NEWTON - 1):
        left = [twice - dot(inv[w], over[w], highest) for w in range(count)]
        inv = [dot(left[w], spread(inv[w]), highest) for w in range(count)]
    rows = up_to(nelec, 8)
    lane = lax.broadcasted_iota(jnp.int32, (1, half), 1)
    row = jnp.zeros((1, half), f32)
    for w in range(count):
        theta = dot(spread(inv[w]), full[w], highest)
        log_part = jnp.zeros((1, 1), f32)
        for g in range(nvec):
            top = tops[g]
            xr = ROOT_DT * jnp.sum(top * theta[:rows], keepdims=True)
            xi = ROOT_DT * jnp.sum(top * theta[pad : pad + rows], keepdims=True)
            field = fields[w, g]
            at = 2 * (w * nvec + g)
            row += jnp.where(lane == at, ROOT_DT * xi, 0.0)
            row += jnp.where(lane == at + 1, ROOT_DT * (field - xr), 0.0)
            log_part += field * xr - 0.5 * (xr * xr - xi * xi)
        row += jnp.where(lane == 2 * count * nvec + w, log_part, 0.0)
    mask = lax.broadcasted_iota(jnp.int32, (SMALL, half), 0) == 0
    small[...] = jnp.where(mask, row, diags[...])


def group_kernel(count, nvec, weights, counts, *refs):
    smalls, out = refs[:-1], refs[-1]
    width = out.shape[1]
    lane = lax.broadcasted_iota(jnp.int32, (1, width), 1)
    per = 2 * count * nvec
    lines = [s[0:1] for s in smalls]
    logs = lines[0]
    for line in lines[1:]:
        logs = logs + line
    row = jnp.zeros((1, width), f32)
    for k, line in enumerate(lines):
        mine = jnp.where(lane < per, line, 0.0)
        row += mine if k == 0 else pltpu.roll(mine, k * per, 1)
    base = per * len(lines)
    for w in range(count):
        log_weight = jnp.sum(jnp.where(lane == per + w, logs, 0.0), axis=1, keepdims=True)
        row += jnp.where(lane == base + w, weights[w] * jnp.exp(log_weight), 0.0)
        row += jnp.where(lane == base + count + w, counts[w].astype(f32), 0.0)
    out[...] = row


def add_pieces(acc, base, at_half, p, pieces, coeff, part, step):
    def add_up(t, _):
        r = pl.multiple_of(t * step, step)
        here = pl.ds(pl.multiple_of(p * part + r, step), step)
        if base is None:
            sums = [None] * len(coeff)
        else:
            sums = [base[n, at_half, here, :] for n in range(len(coeff))]
        for k, piece in enumerate(pieces):
            for g in range(len(coeff[0][k])):
                block = piece[pl.ds(pl.multiple_of(g * part + r, step), step), :]
                for n in range(len(coeff)):
                    more = coeff[n][k][g] * block
                    sums[n] = more if sums[n] is None else sums[n] + more
        for n in range(len(coeff)):
            acc[n, at_half, here, :] = sums[n]
        return 0

    lax.fori_loop(0, part // step, add_up, 0)


def first_kernel(count, nvec, slots, late, zs, swaps, where_at, rows, *refs):
    refs = list(refs)

    def take(n):
        head = refs[:n]
        del refs[:n]
        return head

    early = slots - len(late)
    walks = take(3)
    smalls = take(slots)
    mine = take(2 * early)
    other, joined = take(2)
    acc, diags, source, marks, late_coeff = refs
    me, core = where_at[0], where_at[1]
    per = 2 * count * nvec
    base = per * slots
    width = walks[0].shape[1]
    nelec = width // 2
    norb = walks[0].shape[2]
    half = norb // 2
    part = half // 2
    pad = source.shape[1] // 2

    def row_of(group):
        return group ^ me if swaps else group

    total = jnp.float32(0.0)
    before = jnp.float32(0.0)
    base_count = jnp.float32(0.0)
    for group in range(CORES * zs):
        at = row_of(jnp.int32(group))
        earlier = (group < me).astype(f32)
        for w in range(count):
            weight = rows[at, base + w]
            total += weight
            before += earlier * weight
            base_count += earlier * rows[at, base + count + w]
    lane = lax.broadcasted_iota(jnp.int32, marks.shape, 1)
    mark_row = jnp.zeros(marks.shape, f32)
    for w in range(count):
        before += rows[row_of(me), base + w]
        mark_row += jnp.where(lane == w, before, 0.0)
    marks[...] = (CORES * zs * count) * mark_row / jnp.full(marks.shape, total, f32)

    lines, held = [], []
    for q in range(3):
        group = me + (q - 1)
        exists = (group >= 0) & (group < CORES * zs)
        lines.append(row_of(jnp.where(exists, group, me)))
        held.append(
            [jnp.where(exists, rows[lines[q], base + count + w], 0.0) for w in range(count)]
        )
    begin = base_count
    for w in range(count):
        begin -= held[0][w]
    line = [jnp.int32(0)] * count
    which = [jnp.int32(0)] * count
    place = [jnp.int32(0)] * count
    for q in range(3):
        at = jnp.int32(0) if q == 1 else jnp.where(core == (1 if q == 0 else 0), 1, 2)
        for w in range(count):
            end = begin + held[q][w]
            for j in range(count):
                slot = (me * count + j).astype(f32)
                chosen = (begin <= slot) & (slot < end)
                line[j] = jnp.where(chosen, lines[q], line[j])
                which[j] = jnp.where(chosen, w, which[j])
                place[j] = jnp.where(chosen, at, place[j])
            begin = end
    coeff = []
    for j in range(count):
        for ri in range(2):
            coeff.append(
                [
                    [
                        rows[line[j], slot * per + which[j] * 2 * nvec + 2 * g + ri]
                        for g in range(nvec)
                    ]
                    for slot in range(slots)
                ]
            )
        for k in range(3):

            @pl.when(place[j] == k)
            def _():
                source[j, :nelec] = walks[k][which[j], :nelec]
                source[j, pad : pad + nelec] = walks[k][which[j], nelec:]

        for lo in (nelec, pad + nelec):
            source[j, lo : lo + pad - nelec] = jnp.zeros((pad - nelec, norb), f32)

    for n in range(2 * count):
        for k, slot in enumerate(late):
            for g in range(nvec):
                late_coeff[n, k * nvec + g] = coeff[n][slot][g]
        diag = jnp.zeros((1, half), f32)
        for k in range(slots):
            for g in range(nvec):
                diag += coeff[n][k][g] * smalls[k][g + 1 : g + 2, :]
        diags[n : n + 1] = diag
    now = [[c[k] for k in range(slots) if k not in late] for c in coeff]
    size = nvec * part
    theirs = [other.at[0], other.at[1]]
    theirs += [joined.at[pl.ds(n * size, size)] for n in range(2 * early - 2)]
    for side, pieces in enumerate((mine, theirs)):
        at_half = core if side == 0 else CORES - 1 - core
        for p in range(2):
            add_pieces(acc, None, at_half, p, pieces[p::2], now, part, 16)


def last_kernel(count, nvec, late, where_at, late_coeff, early, diags, source, *refs):
    pieces, (out, acc, a_hi, a_lo) = list(refs[:-4]), refs[-4:]
    if late:
        joined = pieces.pop()
        size = joined.shape[0] // (2 * late)
        pieces += [joined.at[pl.ds(n * size, size)] for n in range(2 * late)]
    core = where_at[1]
    half = early.shape[2]
    part = half // 2
    pad = source.shape[1] // 2
    nelec = out.shape[1] // 2
    coeff = [
        [[late_coeff[n, k * nvec + g] for g in range(nvec)] for k in range(late)]
        for n in range(2 * count)
    ]
    for side in range(2):
        at_half = core if side == 0 else CORES - 1 - core
        for p in range(2):
            at = 2 * late * side + p
            add_pieces(acc, early, at_half, p, pieces[at : at + 2 * late : 2], coeff, part, 16)

    i, j_ = ids(half, half)
    for j in range(count):
        for ri in range(2):
            diag = diags[2 * j + ri : 2 * j + ri + 1]
            square = acc[2 * j + ri, 0]
            turned = square.T
            corner = acc[2 * j + ri, 1]

            def put(value, r, c):
                hi = value.astype(jnp.bfloat16)
                a_hi[j, ri, pl.ds(r, half), pl.ds(c, half)] = hi
                a_lo[j, ri, pl.ds(r, half), pl.ds(c, half)] = (value - hi.astype(f32)).astype(jnp.bfloat16)

            put(jnp.where(i <= j_, square, turned), 0, 0)
            put(jnp.where(i > j_, square, jnp.where(i < j_, turned, diag)), half, half)
            put(corner, 0, half)
            put(corner.T, half, 0)

    series = [source[j] for j in range(count)]
    terms = list(series)
    for degree in range(1, TAYLOR + 1):
        for j in range(count):
            term = terms[j]
            hi = term.astype(jnp.bfloat16)
            lo = (term - hi.astype(f32)).astype(jnp.bfloat16)
            both = jnp.concatenate([hi, lo], axis=0)
            prods = []
            for ri in range(2):
                wide = dot(both, a_hi[j, ri])
                prods.append(wide[: 2 * pad] + wide[2 * pad :] + dot(hi, a_lo[j, ri]))
            real = prods[0][:pad] - prods[1][pad:]
            imag = prods[0][pad:] + prods[1][:pad]
            terms[j] = jnp.concatenate([real, imag], axis=0) / degree
            series[j] = series[j] + terms[j]
    for j in range(count):
        out[j, :nelec] = series[j][:nelec]
        out[j, nelec:] = series[j][pad : pad + nelec]


def join_kernel(*refs):
    size = refs[0].shape[0]
    for n, ref in enumerate(refs[:-1]):
        refs[-1][n * size : (n + 1) * size] = ref[...]


def join(pieces, cost):
    rows, columns = pieces[0].shape
    return pl.pallas_call(
        join_kernel,
        out_shape=jax.ShapeDtypeStruct((len(pieces) * rows, columns), f32),
        in_specs=[VMEM] * len(pieces),
        out_specs=VMEM,
        compiler_params=PARAMS,
        cost_estimate=pl.CostEstimate(flops=cost, bytes_accessed=10, transcendentals=0),
    )(*pieces)


def after(value, *others):
    return lax.optimization_barrier((value, *others))[0]


def on_device(walkers, cholesky, fields, weights, counts):
    count, norb, width = walkers.shape
    nvec = cholesky.shape[0]
    half = norb // 2
    part = half // 2
    groups, shards = lax.axis_size("walk"), lax.axis_size("chol")
    zs = groups // CORES
    across = max(d for d in range(1, shards + 1) if shards % d == 0 and d * d <= shards)
    down = shards // across
    me = lax.axis_index("walk").astype(jnp.int32)
    core = me % CORES
    where_at = jnp.stack([me, core])

    def move(block, dy, dx):
        route = []
        for s in range(shards):
            y, x = divmod(s, across)
            route.append((s, (y + dy) % down * across + (x + dx) % across))
        return lax.ppermute(block, "chol", route)

    def to_core(block):
        return lax.ppermute(block, "walk", [(g, g ^ 1) for g in range(groups)])

    def over_edge(block):
        route = [(g, g + 1) for g in range(1, groups - 1, CORES)]
        return lax.ppermute(block, "walk", route + [(b, a) for a, b in route])

    order = [(dy, dx) for dy in range(down) for dx in range(across)]
    late = [k for k, (dy, dx) in enumerate(order) if dy and dx]
    walk_t = jnp.swapaxes(walkers, 1, 2)

    first, second, other, top, diags = pack(where_at, cholesky, up_to(width // 2, 8))
    got1, got2 = {(0, 0): first}, {(0, 0): second}
    for dx in range(1, across):
        got1[0, dx] = move(first, 0, dx)
    for dy in range(1, down):
        got2[dy, 0] = move(second, dy, 0)

    edge_walk = over_edge(after(walk_t, first))

    pad = up_to(width // 2, 128)
    small = pl.pallas_call(
        prep_kernel,
        out_shape=jax.ShapeDtypeStruct((SMALL, half), f32),
        in_specs=[SMEM] + [VMEM] * 3,
        out_specs=VMEM,
        scratch_shapes=[pltpu.VMEM((count, 2 * pad, norb), f32)],
        compiler_params=PARAMS,
        cost_estimate=pl.CostEstimate(flops=10**10, bytes_accessed=3 * 10**6, transcendentals=0),
    )(fields, walk_t, top, diags)
    smalls = [small if d == (0, 0) else move(small, *d) for d in order]
    for dx in range(1, across):
        got2[0, dx] = move(after(second, small, got1[0, dx]), 0, dx)
    for dy in range(1, down):
        got1[dy, 0] = move(after(first, small, got2[dy, 0]), dy, 0)
    for dy in range(1, down):
        for dx in range(1, across):
            got1[dy, dx] = move(got1[0, dx], dy, 0)
            got2[dy, dx] = move(got2[dy, 0], 0, dx)

    mine = [(got1[d], got2[d]) for d in order]
    joint = [p for k, two in enumerate(mine) for p in two if k and k not in late]
    core_walk = to_core(after(walk_t, small))
    row = pl.pallas_call(
        functools.partial(group_kernel, count, nvec),
        out_shape=jax.ShapeDtypeStruct((1, half), f32),
        in_specs=[SMEM, SMEM] + [VMEM] * shards,
        out_specs=VMEM,
        compiler_params=PARAMS,
        cost_estimate=pl.CostEstimate(flops=K2_COST, bytes_accessed=10, transcendentals=0),
    )(weights, counts, *smalls)
    swaps = groups & (groups - 1) == 0
    if swaps:
        rows = row
        for k in range(groups.bit_length() - 1):
            route = [(g, g ^ 2**k) for g in range(groups)]
            if k == EDGE_STEP:
                rows = after(rows, edge_walk)
            rows = jnp.concatenate([rows, lax.ppermute(rows, "walk", route)], axis=0)
            pair = rows if k < 2 else pair
    else:
        rows = pair = lax.all_gather(row, "walk", axis=0, tiled=True)
    joined = to_core(join([after(p, pair) for p in joint], EARLY_COST))
    my_late = [p for k in late for p in mine[k]]
    their_late = to_core(join(my_late, LATE_COST)) if late else None
    soon = [p for k, two in enumerate(mine) for p in two if k not in late] + [other, joined]
    epad = up_to(width // 2, 16)
    acc, diags, source, marks, late_coeff = pl.pallas_call(
        functools.partial(first_kernel, count, nvec, shards, late, zs, swaps),
        out_shape=(
            jax.ShapeDtypeStruct((2 * count, 2, half, half), f32),
            jax.ShapeDtypeStruct((up_to(2 * count, 8), half), f32),
            jax.ShapeDtypeStruct((count, 2 * epad, norb), f32),
            jax.ShapeDtypeStruct((1, 128), f32),
            jax.ShapeDtypeStruct((2 * count, max(1, len(late)) * nvec), f32),
        ),
        in_specs=[SMEM] * 2 + [VMEM] * (3 + shards + len(soon)),
        out_specs=(VMEM, VMEM, VMEM, VMEM, SMEM),
        compiler_params=PARAMS,
        cost_estimate=pl.CostEstimate(flops=K_COST, bytes_accessed=10, transcendentals=0),
    )(where_at, rows, walk_t, core_walk, edge_walk, *smalls, *soon)

    rest = my_late + ([their_late] if late else [])
    out = pl.pallas_call(
        functools.partial(last_kernel, count, nvec, len(late)),
        out_shape=jax.ShapeDtypeStruct((count, width, norb), f32),
        in_specs=[SMEM, SMEM] + [VMEM] * (3 + len(rest)),
        out_specs=VMEM,
        scratch_shapes=[
            pltpu.VMEM((2 * count, 2, half, half), f32),
            pltpu.VMEM((count, 2, norb, norb), jnp.bfloat16),
            pltpu.VMEM((count, 2, norb, norb), jnp.bfloat16),
        ],
        compiler_params=PARAMS,
        cost_estimate=pl.CostEstimate(flops=10**10, bytes_accessed=10**7, transcendentals=0),
    )(where_at, late_coeff, acc, diags, source, *rest)
    return jnp.swapaxes(out, 1, 2), marks[0, :count]


def solution(mesh):
    in_specs = (
        P("walk", None, None),
        P("chol", None, None),
        P("walk", "chol"),
        P("walk"),
        P("walk"),
    )
    out_specs = (P("walk", None, None), P("walk"))
    return jax.shard_map(
        on_device, mesh=mesh, in_specs=in_specs, out_specs=out_specs, check_vma=False
    )
```

time: 61.8 us -> 45.4 us (0.73)
  waiting for transfers between devices: 24.2 us -> 7.71 us
  starting transfers between devices: 18.8 us -> 20.7 us
  other arithmetic: 1.75 us -> 0.1 us
  Pallas kernels: 14.5 us -> 13.7 us
    ppermute x9, waiting for transfers between devices: 15.5 us -> 3.36 us  [move(): return lax.ppermute(block, 'chol', route)]
    ppermute x7 -> x3, waiting for transfers between devices: 2.54 us -> 0.01 us  [to_core(): return lax.ppermute(block, 'walk', [(g, g ^ 1) for g in range(groups)])]
    ppermute x9, starting transfers between devices: 9.43 us -> 11.9 us  [move(): return lax.ppermute(block, 'chol', route)]
    ppermute x5 -> x4, waiting for transfers between devices: 6.17 us -> 4.35 us  [the longest x3 4.35 us: on_device(): rows = jnp.concatenate([rows, lax.ppermute(rows, 'walk', route)], axis=0)]
    select_n x1 -> x0, other arithmetic: 1.64 us -> none  [packed(): return jnp.where(which == 0, both, vectors[:, :m, m:])]
    pallas_call x2 -> x6, Pallas kernels: 13.9 us -> 13.1 us  [the longest x1 6.58 us: on_device(): pl.pallas_call(functools.partial(last_kernel, count, nvec, len(late)), ou...]
    unnamed x12 -> x10, local copies, waits for them, and re-layouts: 0.92 us -> 1.61 us
    ppermute x5 -> x4, starting transfers between devices: 8.27 us -> 7.64 us  [the longest x3 6.94 us: on_device(): rows = jnp.concatenate([rows, lax.ppermute(rows, 'walk', route)], axis=0)]
  transfers between devices with their start and end apart: 21 -> 16, of which waited for: 11 -> 6; matrix products, arithmetic and copies ran while one was open for 0% -> 1% of each run, Pallas kernels for 10% -> 14%
where the time goes in v1:
time: 45.4 us; the launch traced here: 45.2 us
  starting transfers between devices  20.7 us (46%)
  Pallas kernels  13.7 us (30%)
  waiting for transfers between devices  7.71 us (17%)
  local copies, waits for them, and re-layouts  2.12 us (5%)
  between operations  0.78 us (2%)
    ppermute x9, starting transfers between devices, move(): return lax.ppermute(block, 'chol', route)  11.9 us
    ppermute x3, starting transfers between devices, on_device(): rows = jnp.concatenate([rows, lax.ppermute(rows, 'walk', route)], axis=0)  6.94 us
    pallas_call x1, Pallas kernels, on_device(): pl.pallas_call(functools.partial(last_kernel, count, nvec, len(late)), ou...  6.58 us
    ppermute x3, waiting for transfers between devices, on_device(): rows = jnp.concatenate([rows, lax.ppermute(rows, 'walk', route)], axis=0)  4.35 us
    ppermute x9, waiting for transfers between devices, move(): return lax.ppermute(block, 'chol', route)  3.36 us
    pallas_call x1, Pallas kernels, on_device(): pl.pallas_call(prep_kernel, out_shape=jax.ShapeDtypeStruct((SMALL, half),...  3.12 us
    pallas_call x1, Pallas kernels, on_device(): pl.pallas_call(functools.partial(first_kernel, count, nvec, shards, late,...  2.59 us
    unnamed x10, local copies, waits for them, and re-layouts  1.61 us
  transfers between devices with their start and end apart: 16, of which 6 were waited for; matrix products, arithmetic and copies ran while one was open for 1% of the time, Pallas kernels for 14%

profile of v1, /device:TPU:0, one launch (start us, length us, event | category | flops | bytes accessed | tf_op | source)
XLA Modules:
  0.0 45.2 jit_solution(222547392193003520)
XLA Ops:
  0.7 1.6 %copy-done = f32[2,512,512]{2,1,0:T(8,128)S(1)} copy-done((f32[2,512,512]{2,1,0:T(8,128)S(1)}, f32[2,512,512]{2,1,0:T(8,128)}, u32[]{:S(2)}) %copy-start) | copy-done | bytes 2097176
  2.3 0.7 %shard_map.68 = (f32[256,256]{1,0:T(8,128)S(1)}, f32[256,256]{1,0:T(8,128)S(1)}, f32[2,256,256]{2,1,0:T(8,128)S(1)}, f32[2,104,512]{2,1,0:T(8,128)S(1)}, f32[8,256]{1,0:T(8,128)S(1)}) custom-call(s32[2]{0:T(128)S(1)} %pad_add_fusion.which.where_at, f32[2,512,512]{2,1,0:T(8,128)S(1)} %copy-done), custom_call_target="tpu_custom_call" | custom-call | flops 1000000 | bytes 4000000 | tf_op jit(solution)/shard_map/pallas_call | solution.py:80
  3.0 3.0 %collective-permute-start.10 = (f32[256,256]{1,0:T(8,128)S(1)}, f32[256,256]{1,0:T(8,128)S(1)}, u32[]{:S(2)}, u32[]{:S(2)}) collective-permute-start(f32[256,256]{1,0:T(8,128)S(1)} %get-tuple-element.28.refs_8_), channel_id=1, source_target_pairs={{0,2},{1,3},{2,0},{3,1},{4,6},{5,7},{6,4},{7,5},{8,10},{9,11},{10,... | collective-permute-start | bytes 786440 | tf_op jit(solution)/shard_map/ppermute | solution.py:396
  6.0 1.5 %collective-permute-start.8 = (f32[256,256]{1,0:T(8,128)S(1)}, f32[256,256]{1,0:T(8,128)S(1)}, u32[]{:S(2)}, u32[]{:S(2)}) collective-permute-start(f32[256,256]{1,0:T(8,128)S(1)} %get-tuple-element.29.refs_7_), channel_id=1, source_target_pairs={{0,1},{1,0},{2,3},{3,2},{4,5},{5,4},{6,7},{7,6},{8,9},{9,8},{10,11... | collective-permute-start | bytes 786440 | tf_op jit(solution)/shard_map/ppermute | solution.py:396
  7.5 0.7 %collective-permute-start.3 = (f32[2,200,512]{2,1,0:T(8,128)S(1)}, f32[2,200,512]{2,1,0:T(8,128)S(1)}, u32[]{:S(2)}, u32[]{:S(2)}) collective-permute-start(f32[2,200,512]{2,1,0:T(8,128)S(1)} %bitcast.6), channel_id=1, source_target_pairs={{4,8},{12,16},{20,24},{8,4},{16,12},{24,20},{5,9},{13,17},{21,25},... | collective-permute-start | bytes 2457608 | tf_op jit(solution)/shard_map/ppermute | solution.py:403
  8.3 3.1 %shard_map.69.refs_0_.refs_3_ = f32[8,256]{1,0:T(8,128)S(1)} custom-call(f32[2,2]{1,0:T(2,128)S(1)} %copy-done.2, f32[2,200,512]{2,1,0:T(8,128)S(1)} %bitcast.7, f32[2,104,512]{2,1,0:T(8,128)S(1)} %get-tuple-element.21.tops, f32[8,256]{1,0:T(8,128)S(1)} %get-tuple-element.22.diags), custom_call_target="tpu_custom_call" | custom-call | flops 10000000000 | bytes 3000000 | tf_op jit(solution)/shard_map/pallas_call | solution.py:419
  11.4 0.6 %collective-permute-start = (f32[8,256]{1,0:T(8,128)S(1)}, f32[8,256]{1,0:T(8,128)S(1)}, u32[]{:S(2)}, u32[]{:S(2)}) collective-permute-start(f32[8,256]{1,0:T(8,128)S(1)} %shard_map.69.refs_0_.refs_3_), channel_id=1, source_target_pairs={{0,1},{1,0},{2,3},{3,2},{4,5},{5,4},{6,7},{7,6},{8,9},{9,8},{10,11... | collective-permute-start | bytes 24584 | tf_op jit(solution)/shard_map/ppermute | solution.py:396
  12.4 2.7 %collective-permute-start.2 = (f32[8,256]{1,0:T(8,128)S(1)}, f32[8,256]{1,0:T(8,128)S(1)}, u32[]{:S(2)}, u32[]{:S(2)}) collective-permute-start(f32[8,256]{1,0:T(8,128)S(1)} %shard_map.69.refs_0_.refs_3_), channel_id=1, source_target_pairs={{0,3},{1,2},{2,1},{3,0},{4,7},{5,6},{6,5},{7,4},{8,11},{9,10},{10,... | collective-permute-start | bytes 24584 | tf_op jit(solution)/shard_map/ppermute | solution.py:396
  15.9 1.7 %collective-permute-start.13 = (f32[256,256]{1,0:T(8,128)S(1)}, f32[256,256]{1,0:T(8,128)S(1)}, u32[]{:S(2)}, u32[]{:S(2)}) collective-permute-start(f32[256,256]{1,0:T(8,128)S(1)} %collective-permute-done.8.refs_0_.refs_9_), channel_id=1, source_target_pairs={{0,2},{1,3},{2,0},{3,1},{4,6},{5,7},{6,4},{7,5},{8,10},{9,11},{10,... | collective-permute-start | bytes 786440 | tf_op jit(solution)/shard_map/ppermute | solution.py:396
  17.6 1.5 %collective-permute-start.14 = (f32[256,256]{1,0:T(8,128)S(1)}, f32[256,256]{1,0:T(8,128)S(1)}, u32[]{:S(2)}, u32[]{:S(2)}) collective-permute-start(f32[256,256]{1,0:T(8,128)S(1)} %collective-permute-done.10.refs_3_.refs_12_), channel_id=1, source_target_pairs={{0,1},{1,0},{2,3},{3,2},{4,5},{5,4},{6,7},{7,6},{8,9},{9,8},{10,11... | collective-permute-start | bytes 786440 | tf_op jit(solution)/shard_map/ppermute | solution.py:396
  19.1 0.6 %shard_map.70 = f32[1,256]{1,0:T(1,128)S(1)} custom-call(f32[2]{0:T(128)S(1)} %copy-done.3, s32[2]{0:T(128)S(1)} %copy-done.4, f32[8,256]{1,0:T(8,128)S(1)} %shard_map.69.refs_0_.refs_3_, f32[8,256]{1,0:T(8,128)S(1)} %collective-permute-done.refs_1_.refs_4_, f32[8,256]{1,0:T(8,128)S(1)} %collective-permute-done.1.refs_2_.refs_5_, ...), custom_call_target="tpu_custom_call" | custom-call | flops 4000000000 | bytes 10 | tf_op jit(solution)/shard_map/pallas_call | solution.py:441
  19.7 1.7 %collective-permute-start.4 = (f32[1,256]{1,0:T(1,128)S(1)}, f32[1,256]{1,0:T(1,128)S(1)}, u32[]{:S(2)}, u32[]{:S(2)}) collective-permute-start(f32[1,256]{1,0:T(1,128)S(1)} %shard_map.70), channel_id=1, source_target_pairs={{0,4},{4,0},{8,12},{12,8},{16,20},{20,16},{24,28},{28,24},{1,5},{5... | collective-permute-start | bytes 3080 | tf_op jit(solution)/shard_map/ppermute | solution.py:456
  21.4 0.8 %collective-permute-done.4 = f32[1,256]{1,0:T(1,128)S(1)} collective-permute-done((f32[1,256]{1,0:T(1,128)S(1)}, f32[1,256]{1,0:T(1,128)S(1)}, u32[]{:S(2)}, u32[]{:S(2)}) %collective-permute-start.4) | collective-permute-done | bytes 1056 | tf_op jit(solution)/shard_map/ppermute | solution.py:456
  22.3 1.6 %collective-permute-start.5 = (f32[2,256]{1,0:T(2,128)S(1)}, f32[2,256]{1,0:T(2,128)S(1)}, u32[]{:S(2)}, u32[]{:S(2)}) collective-permute-start(f32[2,256]{1,0:T(2,128)S(1)} %pad_maximum_fusion.2), channel_id=1, source_target_pairs={{0,8},{4,12},{8,0},{12,4},{16,24},{20,28},{24,16},{28,20},{1,9},{5... | collective-permute-start | bytes 6152 | tf_op jit(solution)/shard_map/ppermute | solution.py:456
  23.9 1.9 %collective-permute-done.5 = f32[2,256]{1,0:T(2,128)S(1)} collective-permute-done((f32[2,256]{1,0:T(2,128)S(1)}, f32[2,256]{1,0:T(2,128)S(1)}, u32[]{:S(2)}, u32[]{:S(2)}) %collective-permute-start.5) | collective-permute-done | bytes 2080 | tf_op jit(solution)/shard_map/ppermute | solution.py:456
  26.0 0.6 %collective-permute-start.12 = (f32[1024,256]{1,0:T(8,128)S(1)}, f32[1024,256]{1,0:T(8,128)S(1)}, u32[]{:S(2)}, u32[]{:S(2)}) collective-permute-start(f32[1024,256]{1,0:T(8,128)S(1)} %shard_map.71), channel_id=1, source_target_pairs={{0,4},{4,0},{8,12},{12,8},{16,20},{20,16},{24,28},{28,24},{1,5},{5... | collective-permute-start | bytes 3145736 | tf_op jit(solution)/shard_map/ppermute | solution.py:399
  26.5 2.3 %collective-permute-done.13.refs_0_ = f32[256,256]{1,0:T(8,128)S(1)} collective-permute-done((f32[256,256]{1,0:T(8,128)S(1)}, f32[256,256]{1,0:T(8,128)S(1)}, u32[]{:S(2)}, u32[]{:S(2)}) %collective-permute-start.13) | collective-permute-done | bytes 262176 | tf_op jit(solution)/shard_map/ppermute | solution.py:396
  28.8 0.8 %collective-permute-done.14.refs_1_ = f32[256,256]{1,0:T(8,128)S(1)} collective-permute-done((f32[256,256]{1,0:T(8,128)S(1)}, f32[256,256]{1,0:T(8,128)S(1)}, u32[]{:S(2)}, u32[]{:S(2)}) %collective-permute-start.14) | collective-permute-done | bytes 262176 | tf_op jit(solution)/shard_map/ppermute | solution.py:396
  29.7 0.6 %collective-permute-start.15 = (f32[512,256]{1,0:T(8,128)S(1)}, f32[512,256]{1,0:T(8,128)S(1)}, u32[]{:S(2)}, u32[]{:S(2)}) collective-permute-start(f32[512,256]{1,0:T(8,128)S(1)} %shard_map.73), channel_id=1, source_target_pairs={{0,4},{4,0},{8,12},{12,8},{16,20},{20,16},{24,28},{28,24},{1,5},{5... | collective-permute-start | bytes 1572872 | tf_op jit(solution)/shard_map/ppermute | solution.py:399
  30.3 3.6 %collective-permute-start.6 = (f32[4,256]{1,0:T(4,128)S(1)}, f32[4,256]{1,0:T(4,128)S(1)}, u32[]{:S(2)}, u32[]{:S(2)}) collective-permute-start(f32[4,256]{1,0:T(4,128)S(1)} %pad_maximum_fusion.1), channel_id=1, source_target_pairs={{0,16},{4,20},{8,24},{12,28},{16,0},{20,4},{24,8},{28,12},{1,17},{... | collective-permute-start | bytes 12296 | tf_op jit(solution)/shard_map/ppermute | solution.py:456
  33.9 1.6 %collective-permute-done.6 = f32[4,256]{1,0:T(4,128)S(1)} collective-permute-done((f32[4,256]{1,0:T(4,128)S(1)}, f32[4,256]{1,0:T(4,128)S(1)}, u32[]{:S(2)}, u32[]{:S(2)}) %collective-permute-start.6) | collective-permute-done | bytes 4128 | tf_op jit(solution)/shard_map/ppermute | solution.py:456
  35.5 2.6 %shard_map.72 = (f32[4,2,256,256]{3,2,1,0:T(8,128)S(1)}, f32[8,256]{1,0:T(8,128)S(1)}, f32[2,224,512]{2,1,0:T(8,128)S(1)}, f32[1,128]{1,0:T(1,128)S(1)}, f32[4,2]{1,0:T(4,128)S(1)}) custom-call(s32[2]{0:T(128)S(1)} %pad_add_fusion.which.where_at, f32[8,256]{1,0:T(8,128)S(1)} %pad_maximum_fusion.rows, f32[2,200,512]{2,1,0:T(8,128)S(1)} %bitcast.9, ...), custom_call_target="tpu_custom_call" | custom-call | bytes 10 | tf_op jit(solution)/shard_map/pallas_call | solution.py:465
  38.1 0.5 %slice_bitcast_fusion = f32[2]{0:T(128)} fusion(f32[1,128]{1,0:T(1,128)S(1)} %get-tuple-element.39), kind=kLoop, calls=%fused_computation.4 | loop fusion | bytes 16 | tf_op jit(solution)/shard_map/squeeze | solution.py:494
  38.6 6.6 %shard_map.74 = f32[2,200,512]{2,1,0:T(8,128)} custom-call(s32[2]{0:T(128)S(1)} %pad_add_fusion.which.where_at, f32[4,2]{1,0:T(4,128)S(1)} %get-tuple-element.35.late_coeff, f32[4,2,256,256]{3,2,1,0:T(8,128)S(1)} %get-tuple-element.36.early, f32[8,256]{1,0:T(8,128)S(1)} %get-tuple-element.37.diags, f32[2,224,512]{2,1,0:T(8,128)S(1)} %get-tuple-element.38.source, ...), custom_call_target="tpu_custom_call" | custom-call | flops 10000000000 | bytes 10000000 | tf_op jit(solution)/shard_map/pallas_call | solution.py:481
  (30 shorter events, 1.4 us)
Async XLA Ops:
  0.6 7.6 %copy-start.2 = (f32[2,2]{1,0:T(2,128)S(1)}, f32[2,2]{1,0:T(2,128)}, u32[]{:S(2)}) copy-start(f32[2,2]{1,0:T(2,128)} %fields.1) | copy-start | bytes 52
  0.7 1.6 %copy-start = (f32[2,512,512]{2,1,0:T(8,128)S(1)}, f32[2,512,512]{2,1,0:T(8,128)}, u32[]{:S(2)}) copy-start(f32[2,512,512]{2,1,0:T(8,128)} %vec.1) | copy-start | bytes 6291460
  2.3 5.2 %copy-start.1 = (f32[2,512,200]{1,2,0:T(8,128)S(1)}, f32[2,512,200]{1,2,0:T(8,128)}, u32[]{:S(2)}) copy-start(f32[2,512,200]{1,2,0:T(8,128)} %param.5) | copy-start | bytes 2457604
  3.0 9.3 %collective-permute-start.10 = (f32[256,256]{1,0:T(8,128)S(1)}, f32[256,256]{1,0:T(8,128)S(1)}, u32[]{:S(2)}, u32[]{:S(2)}) collective-permute-start(f32[256,256]{1,0:T(8,128)S(1)} %get-tuple-element.28.refs_8_), channel_id=1, source_target_pairs={{0,2},{1,3},{2,0},{3,1},{4,6},{5,7},{6,4},{7,5},{8,10},{9,11},{10,... | collective-permute-start | bytes 786440 | tf_op jit(solution)/shard_map/ppermute | solution.py:396
  6.0 9.0 %collective-permute-start.8 = (f32[256,256]{1,0:T(8,128)S(1)}, f32[256,256]{1,0:T(8,128)S(1)}, u32[]{:S(2)}, u32[]{:S(2)}) collective-permute-start(f32[256,256]{1,0:T(8,128)S(1)} %get-tuple-element.29.refs_7_), channel_id=1, source_target_pairs={{0,1},{1,0},{2,3},{3,2},{4,5},{5,4},{6,7},{7,6},{8,9},{9,8},{10,11... | collective-permute-start | bytes 786440 | tf_op jit(solution)/shard_map/ppermute | solution.py:396
  7.5 12.2 %collective-permute-start.3 = (f32[2,200,512]{2,1,0:T(8,128)S(1)}, f32[2,200,512]{2,1,0:T(8,128)S(1)}, u32[]{:S(2)}, u32[]{:S(2)}) collective-permute-start(f32[2,200,512]{2,1,0:T(8,128)S(1)} %bitcast.6), channel_id=1, source_target_pairs={{4,8},{12,16},{20,24},{8,4},{16,12},{24,20},{5,9},{13,17},{21,25},... | collective-permute-start | bytes 2457608 | tf_op jit(solution)/shard_map/ppermute | solution.py:403
  8.3 10.8 %copy-start.3 = (f32[2]{0:T(128)S(1)}, f32[2]{0:T(128)}, u32[]{:S(2)}) copy-start(f32[2]{0:T(128)} %weights.1) | copy-start | bytes 28
  8.3 10.8 %copy-start.4 = (s32[2]{0:T(128)S(1)}, s32[2]{0:T(128)}, u32[]{:S(2)}) copy-start(s32[2]{0:T(128)} %counts.1) | copy-start | bytes 28
  11.4 4.1 %collective-permute-start = (f32[8,256]{1,0:T(8,128)S(1)}, f32[8,256]{1,0:T(8,128)S(1)}, u32[]{:S(2)}, u32[]{:S(2)}) collective-permute-start(f32[8,256]{1,0:T(8,128)S(1)} %shard_map.69.refs_0_.refs_3_), channel_id=1, source_target_pairs={{0,1},{1,0},{2,3},{3,2},{4,5},{5,4},{6,7},{7,6},{8,9},{9,8},{10,11... | collective-permute-start | bytes 24584 | tf_op jit(solution)/shard_map/ppermute | solution.py:396
  12.0 3.8 %collective-permute-start.1 = (f32[8,256]{1,0:T(8,128)S(1)}, f32[8,256]{1,0:T(8,128)S(1)}, u32[]{:S(2)}, u32[]{:S(2)}) collective-permute-start(f32[8,256]{1,0:T(8,128)S(1)} %shard_map.69.refs_0_.refs_3_), channel_id=1, source_target_pairs={{0,2},{1,3},{2,0},{3,1},{4,6},{5,7},{6,4},{7,5},{8,10},{9,11},{10,... | collective-permute-start | bytes 24584 | tf_op jit(solution)/shard_map/ppermute | solution.py:396
  12.4 5.2 %collective-permute-start.2 = (f32[8,256]{1,0:T(8,128)S(1)}, f32[8,256]{1,0:T(8,128)S(1)}, u32[]{:S(2)}, u32[]{:S(2)}) collective-permute-start(f32[8,256]{1,0:T(8,128)S(1)} %shard_map.69.refs_0_.refs_3_), channel_id=1, source_target_pairs={{0,3},{1,2},{2,1},{3,0},{4,7},{5,6},{6,5},{7,4},{8,11},{9,10},{10,... | collective-permute-start | bytes 24584 | tf_op jit(solution)/shard_map/ppermute | solution.py:396
  15.0 10.9 %collective-permute-start.11 = (f32[256,256]{1,0:T(8,128)S(1)}, f32[256,256]{1,0:T(8,128)S(1)}, u32[]{:S(2)}, u32[]{:S(2)}) collective-permute-start(f32[256,256]{1,0:T(8,128)S(1)} %get-tuple-element.29.refs_7_), channel_id=1, source_target_pairs={{0,2},{1,3},{2,0},{3,1},{4,6},{5,7},{6,4},{7,5},{8,10},{9,11},{10,... | collective-permute-start | bytes 786440 | tf_op jit(solution)/shard_map/ppermute | solution.py:396
  15.5 10.4 %collective-permute-start.9 = (f32[256,256]{1,0:T(8,128)S(1)}, f32[256,256]{1,0:T(8,128)S(1)}, u32[]{:S(2)}, u32[]{:S(2)}) collective-permute-start(f32[256,256]{1,0:T(8,128)S(1)} %get-tuple-element.28.refs_8_), channel_id=1, source_target_pairs={{0,1},{1,0},{2,3},{3,2},{4,5},{5,4},{6,7},{7,6},{8,9},{9,8},{10,11... | collective-permute-start | bytes 786440 | tf_op jit(solution)/shard_map/ppermute | solution.py:396
  15.9 12.9 %collective-permute-start.13 = (f32[256,256]{1,0:T(8,128)S(1)}, f32[256,256]{1,0:T(8,128)S(1)}, u32[]{:S(2)}, u32[]{:S(2)}) collective-permute-start(f32[256,256]{1,0:T(8,128)S(1)} %collective-permute-done.8.refs_0_.refs_9_), channel_id=1, source_target_pairs={{0,2},{1,3},{2,0},{3,1},{4,6},{5,7},{6,4},{7,5},{8,10},{9,11},{10,... | collective-permute-start | bytes 786440 | tf_op jit(solution)/shard_map/ppermute | solution.py:396
  17.6 12.0 %collective-permute-start.14 = (f32[256,256]{1,0:T(8,128)S(1)}, f32[256,256]{1,0:T(8,128)S(1)}, u32[]{:S(2)}, u32[]{:S(2)}) collective-permute-start(f32[256,256]{1,0:T(8,128)S(1)} %collective-permute-done.10.refs_3_.refs_12_), channel_id=1, source_target_pairs={{0,1},{1,0},{2,3},{3,2},{4,5},{5,4},{6,7},{7,6},{8,9},{9,8},{10,11... | collective-permute-start | bytes 786440 | tf_op jit(solution)/shard_map/ppermute | solution.py:396
  19.7 2.5 %collective-permute-start.4 = (f32[1,256]{1,0:T(1,128)S(1)}, f32[1,256]{1,0:T(1,128)S(1)}, u32[]{:S(2)}, u32[]{:S(2)}) collective-permute-start(f32[1,256]{1,0:T(1,128)S(1)} %shard_map.70), channel_id=1, source_target_pairs={{0,4},{4,0},{8,12},{12,8},{16,20},{20,16},{24,28},{28,24},{1,5},{5... | collective-permute-start | bytes 3080 | tf_op jit(solution)/shard_map/ppermute | solution.py:456
  22.3 3.6 %collective-permute-start.5 = (f32[2,256]{1,0:T(2,128)S(1)}, f32[2,256]{1,0:T(2,128)S(1)}, u32[]{:S(2)}, u32[]{:S(2)}) collective-permute-start(f32[2,256]{1,0:T(2,128)S(1)} %pad_maximum_fusion.2), channel_id=1, source_target_pairs={{0,8},{4,12},{8,0},{12,4},{16,24},{20,28},{24,16},{28,20},{1,9},{5... | collective-permute-start | bytes 6152 | tf_op jit(solution)/shard_map/ppermute | solution.py:456
  25.9 9.6 %collective-permute-start.7 = (f32[2,200,512]{2,1,0:T(8,128)S(1)}, f32[2,200,512]{2,1,0:T(8,128)S(1)}, u32[]{:S(2)}, u32[]{:S(2)}) collective-permute-start(f32[2,200,512]{2,1,0:T(8,128)S(1)} %bitcast.8), channel_id=1, source_target_pairs={{0,4},{4,0},{8,12},{12,8},{16,20},{20,16},{24,28},{28,24},{1,5},{5... | collective-permute-start | bytes 2457608 | tf_op jit(solution)/shard_map/ppermute | solution.py:399
  26.0 9.5 %collective-permute-start.12 = (f32[1024,256]{1,0:T(8,128)S(1)}, f32[1024,256]{1,0:T(8,128)S(1)}, u32[]{:S(2)}, u32[]{:S(2)}) collective-permute-start(f32[1024,256]{1,0:T(8,128)S(1)} %shard_map.71), channel_id=1, source_target_pairs={{0,4},{4,0},{8,12},{12,8},{16,20},{20,16},{24,28},{28,24},{1,5},{5... | collective-permute-start | bytes 3145736 | tf_op jit(solution)/shard_map/ppermute | solution.py:399
  29.7 8.9 %collective-permute-start.15 = (f32[512,256]{1,0:T(8,128)S(1)}, f32[512,256]{1,0:T(8,128)S(1)}, u32[]{:S(2)}, u32[]{:S(2)}) collective-permute-start(f32[512,256]{1,0:T(8,128)S(1)} %shard_map.73), channel_id=1, source_target_pairs={{0,4},{4,0},{8,12},{12,8},{16,20},{20,16},{24,28},{28,24},{1,5},{5... | collective-permute-start | bytes 1572872 | tf_op jit(solution)/shard_map/ppermute | solution.py:399
  30.3 5.2 %collective-permute-start.6 = (f32[4,256]{1,0:T(4,128)S(1)}, f32[4,256]{1,0:T(4,128)S(1)}, u32[]{:S(2)}, u32[]{:S(2)}) collective-permute-start(f32[4,256]{1,0:T(4,128)S(1)} %pad_maximum_fusion.1), channel_id=1, source_target_pairs={{0,16},{4,20},{8,24},{12,28},{16,0},{20,4},{24,8},{28,12},{1,17},{... | collective-permute-start | bytes 12296 | tf_op jit(solution)/shard_map/ppermute | solution.py:456

commit v2 on v1

--- a/solution.py
+++ b/solution.py
@@ -220,12 +220,9 @@
             total += weight
             before += earlier * weight
             base_count += earlier * rows[at, base + count + w]
-    lane = lax.broadcasted_iota(jnp.int32, marks.shape, 1)
-    mark_row = jnp.zeros(marks.shape, f32)
     for w in range(count):
         before += rows[row_of(me), base + w]
-        mark_row += jnp.where(lane == w, before, 0.0)
-    marks[...] = (CORES * zs * count) * mark_row / jnp.full(marks.shape, total, f32)
+        marks[w] = (CORES * zs * count) * before / total
 
     lines, held = [], []
     for q in range(3):
@@ -315,39 +312,49 @@
             add_pieces(acc, early, at_half, p, pieces[at : at + 2 * late : 2], coeff, part, 16)
 
     i, j_ = ids(half, half)
-    for j in range(count):
+
+    def unpack(j):
+        blocks = []
         for ri in range(2):
             diag = diags[2 * j + ri : 2 * j + ri + 1]
             square = acc[2 * j + ri, 0]
             turned = square.T
             corner = acc[2 * j + ri, 1]
-
-            def put(value, r, c):
+            blocks.append(
+                (
+                    jnp.where(i <= j_, square, turned),
+                    corner,
+                    corner.T,
+                    jnp.where(i > j_, square, jnp.where(i < j_, turned, diag)),
+                )
+            )
+        for n in range(4):
+            re, im = blocks[0][n], blocks[1][n]
+            r, c = half * (n // 2), half * (n % 2)
+            for k, value in enumerate((re, im - re, im + re)):
                 hi = value.astype(jnp.bfloat16)
-                a_hi[j, ri, pl.ds(r, half), pl.ds(c, half)] = hi
-                a_lo[j, ri, pl.ds(r, half), pl.ds(c, half)] = (value - hi.astype(f32)).astype(jnp.bfloat16)
-
-            put(jnp.where(i <= j_, square, turned), 0, 0)
-            put(jnp.where(i > j_, square, jnp.where(i < j_, turned, diag)), half, half)
-            put(corner, 0, half)
-            put(corner.T, half, 0)
-
-    series = [source[j] for j in range(count)]
-    terms = list(series)
+                a_hi[j, k, r : r + half, c : c + half] = hi
+                a_lo[j, k, r : r + half, c : c + half] = (value - hi.astype(f32)).astype(jnp.bfloat16)
+
+    terms = [source[j] for j in range(count)]
+    series = list(terms)
+
+    def advance(j, degree):
+        term = terms[j]
+        prods = []
+        for n, left in enumerate((term[:pad] + term[pad:], term[:pad], term[pad:])):
+            hi = left.astype(jnp.bfloat16)
+            lo = (left - hi.astype(f32)).astype(jnp.bfloat16)
+            wide = dot(jnp.concatenate([hi, lo], axis=0), a_hi[j, n])
+            prods.append(wide[:pad] + wide[pad:] + dot(hi, a_lo[j, n]))
+        terms[j] = jnp.concatenate([prods[0] - prods[2], prods[0] + prods[1]], axis=0) / degree
+        series[j] = series[j] + terms[j]
+
+    for j in range(count):
+        unpack(j)
     for degree in range(1, TAYLOR + 1):
         for j in range(count):
-            term = terms[j]
-            hi = term.astype(jnp.bfloat16)
-            lo = (term - hi.astype(f32)).astype(jnp.bfloat16)
-            both = jnp.concatenate([hi, lo], axis=0)
-            prods = []
-            for ri in range(2):
-                wide = dot(both, a_hi[j, ri])
-                prods.append(wide[: 2 * pad] + wide[2 * pad :] + dot(hi, a_lo[j, ri]))
-            real = prods[0][:pad] - prods[1][pad:]
-            imag = prods[0][pad:] + prods[1][:pad]
-            terms[j] = jnp.concatenate([real, imag], axis=0) / degree
-            series[j] = series[j] + terms[j]
+            advance(j, degree)
     for j in range(count):
         out[j, :nelec] = series[j][:nelec]
         out[j, nelec:] = series[j][pad : pad + nelec]
@@ -400,7 +407,8 @@
 
     def over_edge(block):
         route = [(g, g + 1) for g in range(1, groups - 1, CORES)]
-        return lax.ppermute(block, "walk", route + [(b, a) for a, b in route])
+        ends = [(g, g) for g in (0, groups - 1)]
+        return lax.ppermute(block, "walk", route + [(b, a) for a, b in route] + ends)
 
     order = [(dy, dx) for dy in range(down) for dx in range(across)]
     late = [k for k, (dy, dx) in enumerate(order) if dy and dx]
@@ -459,7 +467,7 @@
         rows = pair = lax.all_gather(row, "walk", axis=0, tiled=True)
     joined = to_core(join([after(p, pair) for p in joint], EARLY_COST))
     my_late = [p for k in late for p in mine[k]]
-    their_late = to_core(join(my_late, LATE_COST)) if late else None
+    their_late = to_core(join([after(p, rows) for p in my_late], LATE_COST)) if late else None
     soon = [p for k, two in enumerate(mine) for p in two if k not in late] + [other, joined]
     epad = up_to(width // 2, 16)
     acc, diags, source, marks, late_coeff = pl.pallas_call(
@@ -468,11 +476,11 @@
             jax.ShapeDtypeStruct((2 * count, 2, half, half), f32),
             jax.ShapeDtypeStruct((up_to(2 * count, 8), half), f32),
             jax.ShapeDtypeStruct((count, 2 * epad, norb), f32),
-            jax.ShapeDtypeStruct((1, 128), f32),
+            jax.ShapeDtypeStruct((count,), f32),
             jax.ShapeDtypeStruct((2 * count, max(1, len(late)) * nvec), f32),
         ),
         in_specs=[SMEM] * 2 + [VMEM] * (3 + shards + len(soon)),
-        out_specs=(VMEM, VMEM, VMEM, VMEM, SMEM),
+        out_specs=(VMEM, VMEM, VMEM, SMEM, SMEM),
         compiler_params=PARAMS,
         cost_estimate=pl.CostEstimate(flops=K_COST, bytes_accessed=10, transcendentals=0),
     )(where_at, rows, walk_t, core_walk, edge_walk, *smalls, *soon)
@@ -485,13 +493,13 @@
         out_specs=VMEM,
         scratch_shapes=[
             pltpu.VMEM((2 * count, 2, half, half), f32),
-            pltpu.VMEM((count, 2, norb, norb), jnp.bfloat16),
-            pltpu.VMEM((count, 2, norb, norb), jnp.bfloat16),
+            pltpu.VMEM((count, 3, norb, norb), jnp.bfloat16),
+            pltpu.VMEM((count, 3, norb, norb), jnp.bfloat16),
         ],
         compiler_params=PARAMS,
         cost_estimate=pl.CostEstimate(flops=10**10, bytes_accessed=10**7, transcendentals=0),
     )(where_at, late_coeff, acc, diags, source, *rest)
-    return jnp.swapaxes(out, 1, 2), marks[0, :count]
+    return jnp.swapaxes(out, 1, 2), marks
 
 
 def solution(mesh):

time: 45.4 us -> 41.1 us (0.905)
  waiting for transfers between devices: 7.71 us -> 5.74 us
  starting transfers between devices: 20.7 us -> 19.6 us
  local copies, waits for them, and re-layouts: 2.12 us -> 1.61 us
  Pallas kernels: 13.7 us -> 13.2 us
    ppermute x9, waiting for transfers between devices: 3.36 us -> 0.92 us  [move(): return lax.ppermute(block, 'chol', route)]
    ppermute x3, waiting for transfers between devices: 0.01 us -> 1.85 us  [to_core(): return lax.ppermute(block, 'walk', [(g, g ^ 1) for g in range(groups)])]
    ppermute x3, waiting for transfers between devices: 4.35 us -> 2.97 us  [on_device(): rows = jnp.concatenate([rows, lax.ppermute(rows, 'walk', route)], axis=0)]
    ppermute x9, starting transfers between devices: 11.9 us -> 11.2 us  [move(): return lax.ppermute(block, 'chol', route)]
    squeeze x1 -> x0, local copies, waits for them, and re-layouts: 0.51 us -> none  [on_device(): return (jnp.swapaxes(out, 1, 2), marks[0, :count])]
    pallas_call x1, Pallas kernels: 6.58 us -> 6.08 us  [on_device(): pl.pallas_call(functools.partial(last_kernel, count, nvec, len(late)), ou...]
    ppermute x3, starting transfers between devices: 1.17 us -> 0.71 us  [to_core(): return lax.ppermute(block, 'walk', [(g, g ^ 1) for g in range(groups)])]
  transfers between devices with their start and end apart: 16 -> 16, of which waited for: 6 -> 5; matrix products, arithmetic and copies ran while one was open for 1% -> 0% of each run, Pallas kernels for 14% -> 16%
where the time goes in v2:
time: 41.1 us; the launch traced here: 41 us
  starting transfers between devices  19.6 us (48%)
  Pallas kernels  13.2 us (32%)
  waiting for transfers between devices  5.74 us (14%)
  local copies, waits for them, and re-layouts  1.61 us (4%)
  between operations  0.76 us (2%)
    ppermute x9, starting transfers between devices, move(): return lax.ppermute(block, 'chol', route)  11.2 us
    ppermute x3, starting transfers between devices, on_device(): rows = jnp.concatenate([rows, lax.ppermute(rows, 'walk', route)], axis=0)  6.91 us
    pallas_call x1, Pallas kernels, on_device(): pl.pallas_call(functools.partial(last_kernel, count, nvec, len(late)), ou...  6.08 us
    pallas_call x1, Pallas kernels, on_device(): pl.pallas_call(prep_kernel, out_shape=jax.ShapeDtypeStruct((SMALL, half),...  3.12 us
    ppermute x3, waiting for transfers between devices, on_device(): rows = jnp.concatenate([rows, lax.ppermute(rows, 'walk', route)], axis=0)  2.97 us
    pallas_call x1, Pallas kernels, on_device(): pl.pallas_call(functools.partial(first_kernel, count, nvec, shards, late,...  2.58 us
    ppermute x3, waiting for transfers between devices, to_core(): return lax.ppermute(block, 'walk', [(g, g ^ 1) for g in range(groups)])  1.85 us
    unnamed x10, local copies, waits for them, and re-layouts  1.61 us
  transfers between devices with their start and end apart: 16, of which 5 were waited for; matrix products, arithmetic and copies ran while one was open for 0% of the time, Pallas kernels for 16%

profile of v2, /device:TPU:0, one launch (start us, length us, event | category | flops | bytes accessed | tf_op | source)
XLA Modules:
  0.0 41.0 jit_solution(11256365078065841467)
XLA Ops:
  0.7 1.6 %copy-done = f32[2,512,512]{2,1,0:T(8,128)S(1)} copy-done((f32[2,512,512]{2,1,0:T(8,128)S(1)}, f32[2,512,512]{2,1,0:T(8,128)}, u32[]{:S(2)}) %copy-start) | copy-done | bytes 2097176
  2.3 0.7 %shard_map.68 = (f32[256,256]{1,0:T(8,128)S(1)}, f32[256,256]{1,0:T(8,128)S(1)}, f32[2,256,256]{2,1,0:T(8,128)S(1)}, f32[2,104,512]{2,1,0:T(8,128)S(1)}, f32[8,256]{1,0:T(8,128)S(1)}) custom-call(s32[2]{0:T(128)S(1)} %pad_add_fusion.which.where_at, f32[2,512,512]{2,1,0:T(8,128)S(1)} %copy-done), custom_call_target="tpu_custom_call" | custom-call | flops 1000000 | bytes 4000000 | tf_op jit(solution)/shard_map/pallas_call | solution.py:80
  3.0 3.0 %collective-permute-start.8 = (f32[256,256]{1,0:T(8,128)S(1)}, f32[256,256]{1,0:T(8,128)S(1)}, u32[]{:S(2)}, u32[]{:S(2)}) collective-permute-start(f32[256,256]{1,0:T(8,128)S(1)} %get-tuple-element.31.refs_7_), channel_id=1, source_target_pairs={{0,1},{1,0},{2,3},{3,2},{4,5},{5,4},{6,7},{7,6},{8,9},{9,8},{10,11... | collective-permute-start | bytes 786440 | tf_op jit(solution)/shard_map/ppermute | solution.py:403
  6.0 0.7 %collective-permute-start.3 = (f32[2,200,512]{2,1,0:T(8,128)S(1)}, f32[2,200,512]{2,1,0:T(8,128)S(1)}, u32[]{:S(2)}, u32[]{:S(2)}) collective-permute-start(f32[2,200,512]{2,1,0:T(8,128)S(1)} %bitcast.4), channel_id=1, source_target_pairs={{4,8},{12,16},{20,24},{8,4},{16,12},{24,20},{0,0},{28,28},{5,9},{1... | collective-permute-start | bytes 2457608 | tf_op jit(solution)/shard_map/ppermute | solution.py:411
  6.7 1.6 %collective-permute-start.10 = (f32[256,256]{1,0:T(8,128)S(1)}, f32[256,256]{1,0:T(8,128)S(1)}, u32[]{:S(2)}, u32[]{:S(2)}) collective-permute-start(f32[256,256]{1,0:T(8,128)S(1)} %get-tuple-element.30.refs_8_), channel_id=1, source_target_pairs={{0,2},{1,3},{2,0},{3,1},{4,6},{5,7},{6,4},{7,5},{8,10},{9,11},{10,... | collective-permute-start | bytes 786440 | tf_op jit(solution)/shard_map/ppermute | solution.py:403
  8.3 3.1 %shard_map.69.refs_0_.refs_3_ = f32[8,256]{1,0:T(8,128)S(1)} custom-call(f32[2,2]{1,0:T(2,128)S(1)} %copy-done.2, f32[2,200,512]{2,1,0:T(8,128)S(1)} %bitcast.5, f32[2,104,512]{2,1,0:T(8,128)S(1)} %get-tuple-element.23.tops, f32[8,256]{1,0:T(8,128)S(1)} %get-tuple-element.24.diags), custom_call_target="tpu_custom_call" | custom-call | flops 10000000000 | bytes 3000000 | tf_op jit(solution)/shard_map/pallas_call | solution.py:427
  11.4 0.6 %collective-permute-start = (f32[8,256]{1,0:T(8,128)S(1)}, f32[8,256]{1,0:T(8,128)S(1)}, u32[]{:S(2)}, u32[]{:S(2)}) collective-permute-start(f32[8,256]{1,0:T(8,128)S(1)} %shard_map.69.refs_0_.refs_3_), channel_id=1, source_target_pairs={{0,1},{1,0},{2,3},{3,2},{4,5},{5,4},{6,7},{7,6},{8,9},{9,8},{10,11... | collective-permute-start | bytes 24584 | tf_op jit(solution)/shard_map/ppermute | solution.py:403
  12.0 0.4 collective-permute-start.1
  12.4 2.6 %collective-permute-start.2 = (f32[8,256]{1,0:T(8,128)S(1)}, f32[8,256]{1,0:T(8,128)S(1)}, u32[]{:S(2)}, u32[]{:S(2)}) collective-permute-start(f32[8,256]{1,0:T(8,128)S(1)} %shard_map.69.refs_0_.refs_3_), channel_id=1, source_target_pairs={{0,3},{1,2},{2,1},{3,0},{4,7},{5,6},{6,5},{7,4},{8,11},{9,10},{10,... | collective-permute-start | bytes 24584 | tf_op jit(solution)/shard_map/ppermute | solution.py:403
  15.0 0.5 %collective-permute-start.9 = (f32[256,256]{1,0:T(8,128)S(1)}, f32[256,256]{1,0:T(8,128)S(1)}, u32[]{:S(2)}, u32[]{:S(2)}) collective-permute-start(f32[256,256]{1,0:T(8,128)S(1)} %get-tuple-element.30.refs_8_), channel_id=1, source_target_pairs={{0,1},{1,0},{2,3},{3,2},{4,5},{5,4},{6,7},{7,6},{8,9},{9,8},{10,11... | collective-permute-start | bytes 786440 | tf_op jit(solution)/shard_map/ppermute | solution.py:403
  15.6 0.5 %collective-permute-start.11 = (f32[256,256]{1,0:T(8,128)S(1)}, f32[256,256]{1,0:T(8,128)S(1)}, u32[]{:S(2)}, u32[]{:S(2)}) collective-permute-start(f32[256,256]{1,0:T(8,128)S(1)} %get-tuple-element.31.refs_7_), channel_id=1, source_target_pairs={{0,2},{1,3},{2,0},{3,1},{4,6},{5,7},{6,4},{7,5},{8,10},{9,11},{10,... | collective-permute-start | bytes 786440 | tf_op jit(solution)/shard_map/ppermute | solution.py:403
  16.1 0.9 %collective-permute-done.2.refs_3_.refs_6_ = f32[8,256]{1,0:T(8,128)S(1)} collective-permute-done((f32[8,256]{1,0:T(8,128)S(1)}, f32[8,256]{1,0:T(8,128)S(1)}, u32[]{:S(2)}, u32[]{:S(2)}) %collective-permute-start.2) | collective-permute-done | bytes 8224 | tf_op jit(solution)/shard_map/ppermute | solution.py:403
  17.0 0.6 %shard_map.70 = f32[1,256]{1,0:T(1,128)S(1)} custom-call(f32[2]{0:T(128)S(1)} %copy-done.3, s32[2]{0:T(128)S(1)} %copy-done.4, f32[8,256]{1,0:T(8,128)S(1)} %shard_map.69.refs_0_.refs_3_, f32[8,256]{1,0:T(8,128)S(1)} %collective-permute-done.refs_1_.refs_4_, f32[8,256]{1,0:T(8,128)S(1)} %collective-permute-done.1.refs_2_.refs_5_, ...), custom_call_target="tpu_custom_call" | custom-call | flops 4000000000 | bytes 10 | tf_op jit(solution)/shard_map/pallas_call | solution.py:449
  17.6 2.3 %collective-permute-start.4 = (f32[1,256]{1,0:T(1,128)S(1)}, f32[1,256]{1,0:T(1,128)S(1)}, u32[]{:S(2)}, u32[]{:S(2)}) collective-permute-start(f32[1,256]{1,0:T(1,128)S(1)} %shard_map.70), channel_id=1, source_target_pairs={{0,4},{4,0},{8,12},{12,8},{16,20},{20,16},{24,28},{28,24},{1,5},{5... | collective-permute-start | bytes 3080 | tf_op jit(solution)/shard_map/ppermute | solution.py:464
  19.9 1.5 %collective-permute-start.13 = (f32[256,256]{1,0:T(8,128)S(1)}, f32[256,256]{1,0:T(8,128)S(1)}, u32[]{:S(2)}, u32[]{:S(2)}) collective-permute-start(f32[256,256]{1,0:T(8,128)S(1)} %collective-permute-done.8.refs_0_.refs_9_), channel_id=1, source_target_pairs={{0,2},{1,3},{2,0},{3,1},{4,6},{5,7},{6,4},{7,5},{8,10},{9,11},{10,... | collective-permute-start | bytes 786440 | tf_op jit(solution)/shard_map/ppermute | solution.py:403
  21.4 0.5 %collective-permute-start.14 = (f32[256,256]{1,0:T(8,128)S(1)}, f32[256,256]{1,0:T(8,128)S(1)}, u32[]{:S(2)}, u32[]{:S(2)}) collective-permute-start(f32[256,256]{1,0:T(8,128)S(1)} %collective-permute-done.10.refs_3_.refs_12_), channel_id=1, source_target_pairs={{0,1},{1,0},{2,3},{3,2},{4,5},{5,4},{6,7},{7,6},{8,9},{9,8},{10,11... | collective-permute-start | bytes 786440 | tf_op jit(solution)/shard_map/ppermute | solution.py:403
  22.0 1.8 %collective-permute-start.5 = (f32[2,256]{1,0:T(2,128)S(1)}, f32[2,256]{1,0:T(2,128)S(1)}, u32[]{:S(2)}, u32[]{:S(2)}) collective-permute-start(f32[2,256]{1,0:T(2,128)S(1)} %pad_maximum_fusion.2), channel_id=1, source_target_pairs={{0,8},{4,12},{8,0},{12,4},{16,24},{20,28},{24,16},{28,20},{1,9},{5... | collective-permute-start | bytes 6152 | tf_op jit(solution)/shard_map/ppermute | solution.py:464
  23.8 1.9 %collective-permute-done.5 = f32[2,256]{1,0:T(2,128)S(1)} collective-permute-done((f32[2,256]{1,0:T(2,128)S(1)}, f32[2,256]{1,0:T(2,128)S(1)}, u32[]{:S(2)}, u32[]{:S(2)}) %collective-permute-start.5) | collective-permute-done | bytes 2080 | tf_op jit(solution)/shard_map/ppermute | solution.py:464
  25.7 2.8 %collective-permute-start.6 = (f32[4,256]{1,0:T(4,128)S(1)}, f32[4,256]{1,0:T(4,128)S(1)}, u32[]{:S(2)}, u32[]{:S(2)}) collective-permute-start(f32[4,256]{1,0:T(4,128)S(1)} %pad_maximum_fusion.1), channel_id=1, source_target_pairs={{0,16},{4,20},{8,24},{12,28},{16,0},{20,4},{24,8},{28,12},{1,17},{... | collective-permute-start | bytes 12296 | tf_op jit(solution)/shard_map/ppermute | solution.py:464
  28.5 0.6 %collective-permute-start.12 = (f32[1024,256]{1,0:T(8,128)S(1)}, f32[1024,256]{1,0:T(8,128)S(1)}, u32[]{:S(2)}, u32[]{:S(2)}) collective-permute-start(f32[1024,256]{1,0:T(8,128)S(1)} %shard_map.71), channel_id=1, source_target_pairs={{0,4},{4,0},{8,12},{12,8},{16,20},{20,16},{24,28},{28,24},{1,5},{5... | collective-permute-start | bytes 3145736 | tf_op jit(solution)/shard_map/ppermute | solution.py:406
  29.1 1.1 %collective-permute-done.6 = f32[4,256]{1,0:T(4,128)S(1)} collective-permute-done((f32[4,256]{1,0:T(4,128)S(1)}, f32[4,256]{1,0:T(4,128)S(1)}, u32[]{:S(2)}, u32[]{:S(2)}) %collective-permute-start.6) | collective-permute-done | bytes 4128 | tf_op jit(solution)/shard_map/ppermute | solution.py:464
  30.8 1.5 %collective-permute-done.12.refs_14_ = f32[1024,256]{1,0:T(8,128)S(1)} collective-permute-done((f32[1024,256]{1,0:T(8,128)S(1)}, f32[1024,256]{1,0:T(8,128)S(1)}, u32[]{:S(2)}, u32[]{:S(2)}) %collective-permute-start.12) | collective-permute-done | bytes 1048608 | tf_op jit(solution)/shard_map/ppermute | solution.py:406
  32.3 2.6 %shard_map.72 = (f32[4,2,256,256]{3,2,1,0:T(8,128)S(1)}, f32[8,256]{1,0:T(8,128)S(1)}, f32[2,224,512]{2,1,0:T(8,128)S(1)}, f32[2]{0:T(128)}, f32[4,2]{1,0:T(4,128)S(1)}) custom-call(s32[2]{0:T(128)S(1)} %pad_add_fusion.which.where_at, f32[8,256]{1,0:T(8,128)S(1)} %pad_maximum_fusion.rows, f32[2,200,512]{2,1,0:T(8,128)S(1)} %bitcast.7, ...), custom_call_target="tpu_custom_call" | custom-call | bytes 10 | tf_op jit(solution)/shard_map/pallas_call | solution.py:473
  34.9 6.1 %shard_map.74 = f32[2,200,512]{2,1,0:T(8,128)} custom-call(s32[2]{0:T(128)S(1)} %pad_add_fusion.which.where_at, f32[4,2]{1,0:T(4,128)S(1)} %get-tuple-element.37.late_coeff, f32[4,2,256,256]{3,2,1,0:T(8,128)S(1)} %get-tuple-element.38.early, f32[8,256]{1,0:T(8,128)S(1)} %get-tuple-element.39.diags, f32[2,224,512]{2,1,0:T(8,128)S(1)} %get-tuple-element.40.source, ...), custom_call_target="tpu_custom_call" | custom-call | flops 10000000000 | bytes 10000000 | tf_op jit(solution)/shard_map/pallas_call | solution.py:489
  (29 shorter events, 0.7 us)
Async XLA Ops:
  0.6 7.7 %copy-start.2 = (f32[2,2]{1,0:T(2,128)S(1)}, f32[2,2]{1,0:T(2,128)}, u32[]{:S(2)}) copy-start(f32[2,2]{1,0:T(2,128)} %fields.1) | copy-start | bytes 52
  0.7 1.6 %copy-start = (f32[2,512,512]{2,1,0:T(8,128)S(1)}, f32[2,512,512]{2,1,0:T(8,128)}, u32[]{:S(2)}) copy-start(f32[2,512,512]{2,1,0:T(8,128)} %vec.1) | copy-start | bytes 6291460
  2.3 3.7 %copy-start.1 = (f32[2,512,200]{1,2,0:T(8,128)S(1)}, f32[2,512,200]{1,2,0:T(8,128)}, u32[]{:S(2)}) copy-start(f32[2,512,200]{1,2,0:T(8,128)} %param.5) | copy-start | bytes 2457604
  3.0 9.4 %collective-permute-start.8 = (f32[256,256]{1,0:T(8,128)S(1)}, f32[256,256]{1,0:T(8,128)S(1)}, u32[]{:S(2)}, u32[]{:S(2)}) collective-permute-start(f32[256,256]{1,0:T(8,128)S(1)} %get-tuple-element.31.refs_7_), channel_id=1, source_target_pairs={{0,1},{1,0},{2,3},{3,2},{4,5},{5,4},{6,7},{7,6},{8,9},{9,8},{10,11... | collective-permute-start | bytes 786440 | tf_op jit(solution)/shard_map/ppermute | solution.py:403
  6.0 11.6 %collective-permute-start.3 = (f32[2,200,512]{2,1,0:T(8,128)S(1)}, f32[2,200,512]{2,1,0:T(8,128)S(1)}, u32[]{:S(2)}, u32[]{:S(2)}) collective-permute-start(f32[2,200,512]{2,1,0:T(8,128)S(1)} %bitcast.4), channel_id=1, source_target_pairs={{4,8},{12,16},{20,24},{8,4},{16,12},{24,20},{0,0},{28,28},{5,9},{1... | collective-permute-start | bytes 2457608 | tf_op jit(solution)/shard_map/ppermute | solution.py:411
  6.7 8.3 %collective-permute-start.10 = (f32[256,256]{1,0:T(8,128)S(1)}, f32[256,256]{1,0:T(8,128)S(1)}, u32[]{:S(2)}, u32[]{:S(2)}) collective-permute-start(f32[256,256]{1,0:T(8,128)S(1)} %get-tuple-element.30.refs_8_), channel_id=1, source_target_pairs={{0,2},{1,3},{2,0},{3,1},{4,6},{5,7},{6,4},{7,5},{8,10},{9,11},{10,... | collective-permute-start | bytes 786440 | tf_op jit(solution)/shard_map/ppermute | solution.py:403
  8.3 8.6 %copy-start.3 = (f32[2]{0:T(128)S(1)}, f32[2]{0:T(128)}, u32[]{:S(2)}) copy-start(f32[2]{0:T(128)} %weights.1) | copy-start | bytes 28
  8.3 8.6 %copy-start.4 = (s32[2]{0:T(128)S(1)}, s32[2]{0:T(128)}, u32[]{:S(2)}) copy-start(s32[2]{0:T(128)} %counts.1) | copy-start | bytes 28
  11.4 4.1 %collective-permute-start = (f32[8,256]{1,0:T(8,128)S(1)}, f32[8,256]{1,0:T(8,128)S(1)}, u32[]{:S(2)}, u32[]{:S(2)}) collective-permute-start(f32[8,256]{1,0:T(8,128)S(1)} %shard_map.69.refs_0_.refs_3_), channel_id=1, source_target_pairs={{0,1},{1,0},{2,3},{3,2},{4,5},{5,4},{6,7},{7,6},{8,9},{9,8},{10,11... | collective-permute-start | bytes 24584 | tf_op jit(solution)/shard_map/ppermute | solution.py:403
  12.0 4.0 %collective-permute-start.1 = (f32[8,256]{1,0:T(8,128)S(1)}, f32[8,256]{1,0:T(8,128)S(1)}, u32[]{:S(2)}, u32[]{:S(2)}) collective-permute-start(f32[8,256]{1,0:T(8,128)S(1)} %shard_map.69.refs_0_.refs_3_), channel_id=1, source_target_pairs={{0,2},{1,3},{2,0},{3,1},{4,6},{5,7},{6,4},{7,5},{8,10},{9,11},{10,... | collective-permute-start | bytes 24584 | tf_op jit(solution)/shard_map/ppermute | solution.py:403
  12.4 4.6 %collective-permute-start.2 = (f32[8,256]{1,0:T(8,128)S(1)}, f32[8,256]{1,0:T(8,128)S(1)}, u32[]{:S(2)}, u32[]{:S(2)}) collective-permute-start(f32[8,256]{1,0:T(8,128)S(1)} %shard_map.69.refs_0_.refs_3_), channel_id=1, source_target_pairs={{0,3},{1,2},{2,1},{3,0},{4,7},{5,6},{6,5},{7,4},{8,11},{9,10},{10,... | collective-permute-start | bytes 24584 | tf_op jit(solution)/shard_map/ppermute | solution.py:403
  15.0 13.4 %collective-permute-start.9 = (f32[256,256]{1,0:T(8,128)S(1)}, f32[256,256]{1,0:T(8,128)S(1)}, u32[]{:S(2)}, u32[]{:S(2)}) collective-permute-start(f32[256,256]{1,0:T(8,128)S(1)} %get-tuple-element.30.refs_8_), channel_id=1, source_target_pairs={{0,1},{1,0},{2,3},{3,2},{4,5},{5,4},{6,7},{7,6},{8,9},{9,8},{10,11... | collective-permute-start | bytes 786440 | tf_op jit(solution)/shard_map/ppermute | solution.py:403
  15.6 12.9 %collective-permute-start.11 = (f32[256,256]{1,0:T(8,128)S(1)}, f32[256,256]{1,0:T(8,128)S(1)}, u32[]{:S(2)}, u32[]{:S(2)}) collective-permute-start(f32[256,256]{1,0:T(8,128)S(1)} %get-tuple-element.31.refs_7_), channel_id=1, source_target_pairs={{0,2},{1,3},{2,0},{3,1},{4,6},{5,7},{6,4},{7,5},{8,10},{9,11},{10,... | collective-permute-start | bytes 786440 | tf_op jit(solution)/shard_map/ppermute | solution.py:403
  17.6 4.4 %collective-permute-start.4 = (f32[1,256]{1,0:T(1,128)S(1)}, f32[1,256]{1,0:T(1,128)S(1)}, u32[]{:S(2)}, u32[]{:S(2)}) collective-permute-start(f32[1,256]{1,0:T(1,128)S(1)} %shard_map.70), channel_id=1, source_target_pairs={{0,4},{4,0},{8,12},{12,8},{16,20},{20,16},{24,28},{28,24},{1,5},{5... | collective-permute-start | bytes 3080 | tf_op jit(solution)/shard_map/ppermute | solution.py:464
  19.9 10.3 %collective-permute-start.13 = (f32[256,256]{1,0:T(8,128)S(1)}, f32[256,256]{1,0:T(8,128)S(1)}, u32[]{:S(2)}, u32[]{:S(2)}) collective-permute-start(f32[256,256]{1,0:T(8,128)S(1)} %collective-permute-done.8.refs_0_.refs_9_), channel_id=1, source_target_pairs={{0,2},{1,3},{2,0},{3,1},{4,6},{5,7},{6,4},{7,5},{8,10},{9,11},{10,... | collective-permute-start | bytes 786440 | tf_op jit(solution)/shard_map/ppermute | solution.py:403
  21.4 8.8 %collective-permute-start.14 = (f32[256,256]{1,0:T(8,128)S(1)}, f32[256,256]{1,0:T(8,128)S(1)}, u32[]{:S(2)}, u32[]{:S(2)}) collective-permute-start(f32[256,256]{1,0:T(8,128)S(1)} %collective-permute-done.10.refs_3_.refs_12_), channel_id=1, source_target_pairs={{0,1},{1,0},{2,3},{3,2},{4,5},{5,4},{6,7},{7,6},{8,9},{9,8},{10,11... | collective-permute-start | bytes 786440 | tf_op jit(solution)/shard_map/ppermute | solution.py:403
  22.0 3.7 %collective-permute-start.5 = (f32[2,256]{1,0:T(2,128)S(1)}, f32[2,256]{1,0:T(2,128)S(1)}, u32[]{:S(2)}, u32[]{:S(2)}) collective-permute-start(f32[2,256]{1,0:T(2,128)S(1)} %pad_maximum_fusion.2), channel_id=1, source_target_pairs={{0,8},{4,12},{8,0},{12,4},{16,24},{20,28},{24,16},{28,20},{1,9},{5... | collective-permute-start | bytes 6152 | tf_op jit(solution)/shard_map/ppermute | solution.py:464
  25.7 4.6 %collective-permute-start.6 = (f32[4,256]{1,0:T(4,128)S(1)}, f32[4,256]{1,0:T(4,128)S(1)}, u32[]{:S(2)}, u32[]{:S(2)}) collective-permute-start(f32[4,256]{1,0:T(4,128)S(1)} %pad_maximum_fusion.1), channel_id=1, source_target_pairs={{0,16},{4,20},{8,24},{12,28},{16,0},{20,4},{24,8},{28,12},{1,17},{... | collective-permute-start | bytes 12296 | tf_op jit(solution)/shard_map/ppermute | solution.py:464
  28.5 2.3 %collective-permute-start.7 = (f32[2,200,512]{2,1,0:T(8,128)S(1)}, f32[2,200,512]{2,1,0:T(8,128)S(1)}, u32[]{:S(2)}, u32[]{:S(2)}) collective-permute-start(f32[2,200,512]{2,1,0:T(8,128)S(1)} %bitcast.6), channel_id=1, source_target_pairs={{0,4},{4,0},{8,12},{12,8},{16,20},{20,16},{24,28},{28,24},{1,5},{5... | collective-permute-start | bytes 2457608 | tf_op jit(solution)/shard_map/ppermute | solution.py:406
  28.5 3.7 %collective-permute-start.12 = (f32[1024,256]{1,0:T(8,128)S(1)}, f32[1024,256]{1,0:T(8,128)S(1)}, u32[]{:S(2)}, u32[]{:S(2)}) collective-permute-start(f32[1024,256]{1,0:T(8,128)S(1)} %shard_map.71), channel_id=1, source_target_pairs={{0,4},{4,0},{8,12},{12,8},{16,20},{20,16},{24,28},{28,24},{1,5},{5... | collective-permute-start | bytes 3145736 | tf_op jit(solution)/shard_map/ppermute | solution.py:406
  30.3 4.6 %collective-permute-start.15 = (f32[512,256]{1,0:T(8,128)S(1)}, f32[512,256]{1,0:T(8,128)S(1)}, u32[]{:S(2)}, u32[]{:S(2)}) collective-permute-start(f32[512,256]{1,0:T(8,128)S(1)} %shard_map.73), channel_id=1, source_target_pairs={{0,4},{4,0},{8,12},{12,8},{16,20},{20,16},{24,28},{28,24},{1,5},{5... | collective-permute-start | bytes 1572872 | tf_op jit(solution)/shard_map/ppermute | solution.py:406

commit v3 on v2

--- a/solution.py
+++ b/solution.py
@@ -179,7 +179,7 @@
             acc[n, at_half, here, :] = sums[n]
         return 0
 
-    lax.fori_loop(0, part // step, add_up, 0)
+    lax.fori_loop(0, part // step, add_up, 0, unroll=True)
 
 
 def first_kernel(count, nvec, slots, late, zs, swaps, where_at, rows, *refs):
@@ -287,7 +287,7 @@
     for side, pieces in enumerate((mine, theirs)):
         at_half = core if side == 0 else CORES - 1 - core
         for p in range(2):
-            add_pieces(acc, None, at_half, p, pieces[p::2], now, part, 16)
+            add_pieces(acc, None, at_half, p, pieces[p::2], now, part, 32)
 
 
 def last_kernel(count, nvec, late, where_at, late_coeff, early, diags, source, *refs):
@@ -309,7 +309,7 @@
         at_half = core if side == 0 else CORES - 1 - core
         for p in range(2):
             at = 2 * late * side + p
-            add_pieces(acc, early, at_half, p, pieces[at : at + 2 * late : 2], coeff, part, 16)
+            add_pieces(acc, early, at_half, p, pieces[at : at + 2 * late : 2], coeff, part, 32)
 
     i, j_ = ids(half, half)
 

time: 41.1 us -> 40.3 us (0.981)
  Pallas kernels: 13.2 us -> 12.4 us
    pallas_call x1, Pallas kernels: 2.58 us -> 1.91 us  [on_device(): pl.pallas_call(functools.partial(first_kernel, count, nvec, shards, late,...]
  transfers between devices with their start and end apart: 16 -> 16, of which waited for: 5 -> 5; matrix products, arithmetic and copies ran while one was open for 0% -> 0% of each run, Pallas kernels for 16% -> 14%
where the time goes in v3:
time: 40.3 us; the launch traced here: 40.2 us
  starting transfers between devices  19.6 us (49%)
  Pallas kernels  12.4 us (31%)
  waiting for transfers between devices  5.74 us (14%)
  local copies, waits for them, and re-layouts  1.61 us (4%)
  between operations  0.76 us (2%)
    ppermute x9, starting transfers between devices, move(): return lax.ppermute(block, 'chol', route)  11.2 us
    ppermute x3, starting transfers between devices, on_device(): rows = jnp.concatenate([rows, lax.ppermute(rows, 'walk', route)], axis=0)  6.91 us
    pallas_call x1, Pallas kernels, on_device(): pl.pallas_call(functools.partial(last_kernel, count, nvec, len(late)), ou...  5.93 us
    pallas_call x1, Pallas kernels, on_device(): pl.pallas_call(prep_kernel, out_shape=jax.ShapeDtypeStruct((SMALL, half),...  3.12 us
    ppermute x3, waiting for transfers between devices, on_device(): rows = jnp.concatenate([rows, lax.ppermute(rows, 'walk', route)], axis=0)  2.97 us
    pallas_call x1, Pallas kernels, on_device(): pl.pallas_call(functools.partial(first_kernel, count, nvec, shards, late,...  1.91 us
    ppermute x3, waiting for transfers between devices, to_core(): return lax.ppermute(block, 'walk', [(g, g ^ 1) for g in range(groups)])  1.85 us
    unnamed x10, local copies, waits for them, and re-layouts  1.61 us
  transfers between devices with their start and end apart: 16, of which 5 were waited for; matrix products, arithmetic and copies ran while one was open for 0% of the time, Pallas kernels for 14%

profile of v3, /device:TPU:0, one launch (start us, length us, event | category | flops | bytes accessed | tf_op | source)
XLA Modules:
  0.0 40.2 jit_solution(17848490289164150751)
XLA Ops:
  0.7 1.6 %copy-done = f32[2,512,512]{2,1,0:T(8,128)S(1)} copy-done((f32[2,512,512]{2,1,0:T(8,128)S(1)}, f32[2,512,512]{2,1,0:T(8,128)}, u32[]{:S(2)}) %copy-start) | copy-done | bytes 2097176
  2.3 0.7 %shard_map.68 = (f32[256,256]{1,0:T(8,128)S(1)}, f32[256,256]{1,0:T(8,128)S(1)}, f32[2,256,256]{2,1,0:T(8,128)S(1)}, f32[2,104,512]{2,1,0:T(8,128)S(1)}, f32[8,256]{1,0:T(8,128)S(1)}) custom-call(s32[2]{0:T(128)S(1)} %pad_add_fusion.which.where_at, f32[2,512,512]{2,1,0:T(8,128)S(1)} %copy-done), custom_call_target="tpu_custom_call" | custom-call | flops 1000000 | bytes 4000000 | tf_op jit(solution)/shard_map/pallas_call | solution.py:80
  3.0 3.0 %collective-permute-start.8 = (f32[256,256]{1,0:T(8,128)S(1)}, f32[256,256]{1,0:T(8,128)S(1)}, u32[]{:S(2)}, u32[]{:S(2)}) collective-permute-start(f32[256,256]{1,0:T(8,128)S(1)} %get-tuple-element.31.refs_7_), channel_id=1, source_target_pairs={{0,1},{1,0},{2,3},{3,2},{4,5},{5,4},{6,7},{7,6},{8,9},{9,8},{10,11... | collective-permute-start | bytes 786440 | tf_op jit(solution)/shard_map/ppermute | solution.py:403
  6.0 0.7 %collective-permute-start.3 = (f32[2,200,512]{2,1,0:T(8,128)S(1)}, f32[2,200,512]{2,1,0:T(8,128)S(1)}, u32[]{:S(2)}, u32[]{:S(2)}) collective-permute-start(f32[2,200,512]{2,1,0:T(8,128)S(1)} %bitcast.4), channel_id=1, source_target_pairs={{4,8},{12,16},{20,24},{8,4},{16,12},{24,20},{0,0},{28,28},{5,9},{1... | collective-permute-start | bytes 2457608 | tf_op jit(solution)/shard_map/ppermute | solution.py:411
  6.7 1.6 %collective-permute-start.10 = (f32[256,256]{1,0:T(8,128)S(1)}, f32[256,256]{1,0:T(8,128)S(1)}, u32[]{:S(2)}, u32[]{:S(2)}) collective-permute-start(f32[256,256]{1,0:T(8,128)S(1)} %get-tuple-element.30.refs_8_), channel_id=1, source_target_pairs={{0,2},{1,3},{2,0},{3,1},{4,6},{5,7},{6,4},{7,5},{8,10},{9,11},{10,... | collective-permute-start | bytes 786440 | tf_op jit(solution)/shard_map/ppermute | solution.py:403
  8.3 3.1 %shard_map.69.refs_0_.refs_3_ = f32[8,256]{1,0:T(8,128)S(1)} custom-call(f32[2,2]{1,0:T(2,128)S(1)} %copy-done.2, f32[2,200,512]{2,1,0:T(8,128)S(1)} %bitcast.5, f32[2,104,512]{2,1,0:T(8,128)S(1)} %get-tuple-element.23.tops, f32[8,256]{1,0:T(8,128)S(1)} %get-tuple-element.24.diags), custom_call_target="tpu_custom_call" | custom-call | flops 10000000000 | bytes 3000000 | tf_op jit(solution)/shard_map/pallas_call | solution.py:427
  11.4 0.6 %collective-permute-start = (f32[8,256]{1,0:T(8,128)S(1)}, f32[8,256]{1,0:T(8,128)S(1)}, u32[]{:S(2)}, u32[]{:S(2)}) collective-permute-start(f32[8,256]{1,0:T(8,128)S(1)} %shard_map.69.refs_0_.refs_3_), channel_id=1, source_target_pairs={{0,1},{1,0},{2,3},{3,2},{4,5},{5,4},{6,7},{7,6},{8,9},{9,8},{10,11... | collective-permute-start | bytes 24584 | tf_op jit(solution)/shard_map/ppermute | solution.py:403
  12.0 0.4 collective-permute-start.1
  12.4 2.6 %collective-permute-start.2 = (f32[8,256]{1,0:T(8,128)S(1)}, f32[8,256]{1,0:T(8,128)S(1)}, u32[]{:S(2)}, u32[]{:S(2)}) collective-permute-start(f32[8,256]{1,0:T(8,128)S(1)} %shard_map.69.refs_0_.refs_3_), channel_id=1, source_target_pairs={{0,3},{1,2},{2,1},{3,0},{4,7},{5,6},{6,5},{7,4},{8,11},{9,10},{10,... | collective-permute-start | bytes 24584 | tf_op jit(solution)/shard_map/ppermute | solution.py:403
  15.0 0.5 %collective-permute-start.9 = (f32[256,256]{1,0:T(8,128)S(1)}, f32[256,256]{1,0:T(8,128)S(1)}, u32[]{:S(2)}, u32[]{:S(2)}) collective-permute-start(f32[256,256]{1,0:T(8,128)S(1)} %get-tuple-element.30.refs_8_), channel_id=1, source_target_pairs={{0,1},{1,0},{2,3},{3,2},{4,5},{5,4},{6,7},{7,6},{8,9},{9,8},{10,11... | collective-permute-start | bytes 786440 | tf_op jit(solution)/shard_map/ppermute | solution.py:403
  15.6 0.5 %collective-permute-start.11 = (f32[256,256]{1,0:T(8,128)S(1)}, f32[256,256]{1,0:T(8,128)S(1)}, u32[]{:S(2)}, u32[]{:S(2)}) collective-permute-start(f32[256,256]{1,0:T(8,128)S(1)} %get-tuple-element.31.refs_7_), channel_id=1, source_target_pairs={{0,2},{1,3},{2,0},{3,1},{4,6},{5,7},{6,4},{7,5},{8,10},{9,11},{10,... | collective-permute-start | bytes 786440 | tf_op jit(solution)/shard_map/ppermute | solution.py:403
  16.1 0.9 %collective-permute-done.2.refs_3_.refs_6_ = f32[8,256]{1,0:T(8,128)S(1)} collective-permute-done((f32[8,256]{1,0:T(8,128)S(1)}, f32[8,256]{1,0:T(8,128)S(1)}, u32[]{:S(2)}, u32[]{:S(2)}) %collective-permute-start.2) | collective-permute-done | bytes 8224 | tf_op jit(solution)/shard_map/ppermute | solution.py:403
  17.0 0.6 %shard_map.70 = f32[1,256]{1,0:T(1,128)S(1)} custom-call(f32[2]{0:T(128)S(1)} %copy-done.3, s32[2]{0:T(128)S(1)} %copy-done.4, f32[8,256]{1,0:T(8,128)S(1)} %shard_map.69.refs_0_.refs_3_, f32[8,256]{1,0:T(8,128)S(1)} %collective-permute-done.refs_1_.refs_4_, f32[8,256]{1,0:T(8,128)S(1)} %collective-permute-done.1.refs_2_.refs_5_, ...), custom_call_target="tpu_custom_call" | custom-call | flops 4000000000 | bytes 10 | tf_op jit(solution)/shard_map/pallas_call | solution.py:449
  17.6 2.3 %collective-permute-start.4 = (f32[1,256]{1,0:T(1,128)S(1)}, f32[1,256]{1,0:T(1,128)S(1)}, u32[]{:S(2)}, u32[]{:S(2)}) collective-permute-start(f32[1,256]{1,0:T(1,128)S(1)} %shard_map.70), channel_id=1, source_target_pairs={{0,4},{4,0},{8,12},{12,8},{16,20},{20,16},{24,28},{28,24},{1,5},{5... | collective-permute-start | bytes 3080 | tf_op jit(solution)/shard_map/ppermute | solution.py:464
  19.9 1.5 %collective-permute-start.13 = (f32[256,256]{1,0:T(8,128)S(1)}, f32[256,256]{1,0:T(8,128)S(1)}, u32[]{:S(2)}, u32[]{:S(2)}) collective-permute-start(f32[256,256]{1,0:T(8,128)S(1)} %collective-permute-done.8.refs_0_.refs_9_), channel_id=1, source_target_pairs={{0,2},{1,3},{2,0},{3,1},{4,6},{5,7},{6,4},{7,5},{8,10},{9,11},{10,... | collective-permute-start | bytes 786440 | tf_op jit(solution)/shard_map/ppermute | solution.py:403
  21.4 0.5 %collective-permute-start.14 = (f32[256,256]{1,0:T(8,128)S(1)}, f32[256,256]{1,0:T(8,128)S(1)}, u32[]{:S(2)}, u32[]{:S(2)}) collective-permute-start(f32[256,256]{1,0:T(8,128)S(1)} %collective-permute-done.10.refs_3_.refs_12_), channel_id=1, source_target_pairs={{0,1},{1,0},{2,3},{3,2},{4,5},{5,4},{6,7},{7,6},{8,9},{9,8},{10,11... | collective-permute-start | bytes 786440 | tf_op jit(solution)/shard_map/ppermute | solution.py:403
  22.0 1.8 %collective-permute-start.5 = (f32[2,256]{1,0:T(2,128)S(1)}, f32[2,256]{1,0:T(2,128)S(1)}, u32[]{:S(2)}, u32[]{:S(2)}) collective-permute-start(f32[2,256]{1,0:T(2,128)S(1)} %pad_maximum_fusion.2), channel_id=1, source_target_pairs={{0,8},{4,12},{8,0},{12,4},{16,24},{20,28},{24,16},{28,20},{1,9},{5... | collective-permute-start | bytes 6152 | tf_op jit(solution)/shard_map/ppermute | solution.py:464
  23.8 1.9 %collective-permute-done.5 = f32[2,256]{1,0:T(2,128)S(1)} collective-permute-done((f32[2,256]{1,0:T(2,128)S(1)}, f32[2,256]{1,0:T(2,128)S(1)}, u32[]{:S(2)}, u32[]{:S(2)}) %collective-permute-start.5) | collective-permute-done | bytes 2080 | tf_op jit(solution)/shard_map/ppermute | solution.py:464
  25.7 2.8 %collective-permute-start.6 = (f32[4,256]{1,0:T(4,128)S(1)}, f32[4,256]{1,0:T(4,128)S(1)}, u32[]{:S(2)}, u32[]{:S(2)}) collective-permute-start(f32[4,256]{1,0:T(4,128)S(1)} %pad_maximum_fusion.1), channel_id=1, source_target_pairs={{0,16},{4,20},{8,24},{12,28},{16,0},{20,4},{24,8},{28,12},{1,17},{... | collective-permute-start | bytes 12296 | tf_op jit(solution)/shard_map/ppermute | solution.py:464
  28.5 0.6 %collective-permute-start.12 = (f32[1024,256]{1,0:T(8,128)S(1)}, f32[1024,256]{1,0:T(8,128)S(1)}, u32[]{:S(2)}, u32[]{:S(2)}) collective-permute-start(f32[1024,256]{1,0:T(8,128)S(1)} %shard_map.71), channel_id=1, source_target_pairs={{0,4},{4,0},{8,12},{12,8},{16,20},{20,16},{24,28},{28,24},{1,5},{5... | collective-permute-start | bytes 3145736 | tf_op jit(solution)/shard_map/ppermute | solution.py:406
  29.1 1.1 %collective-permute-done.6 = f32[4,256]{1,0:T(4,128)S(1)} collective-permute-done((f32[4,256]{1,0:T(4,128)S(1)}, f32[4,256]{1,0:T(4,128)S(1)}, u32[]{:S(2)}, u32[]{:S(2)}) %collective-permute-start.6) | collective-permute-done | bytes 4128 | tf_op jit(solution)/shard_map/ppermute | solution.py:464
  30.8 1.5 %collective-permute-done.12.refs_14_ = f32[1024,256]{1,0:T(8,128)S(1)} collective-permute-done((f32[1024,256]{1,0:T(8,128)S(1)}, f32[1024,256]{1,0:T(8,128)S(1)}, u32[]{:S(2)}, u32[]{:S(2)}) %collective-permute-start.12) | collective-permute-done | bytes 1048608 | tf_op jit(solution)/shard_map/ppermute | solution.py:406
  32.3 1.9 %shard_map.72 = (f32[4,2,256,256]{3,2,1,0:T(8,128)S(1)}, f32[8,256]{1,0:T(8,128)S(1)}, f32[2,224,512]{2,1,0:T(8,128)S(1)}, f32[2]{0:T(128)}, f32[4,2]{1,0:T(4,128)S(1)}) custom-call(s32[2]{0:T(128)S(1)} %pad_add_fusion.which.where_at, f32[8,256]{1,0:T(8,128)S(1)} %pad_maximum_fusion.rows, f32[2,200,512]{2,1,0:T(8,128)S(1)} %bitcast.7, ...), custom_call_target="tpu_custom_call" | custom-call | bytes 10 | tf_op jit(solution)/shard_map/pallas_call | solution.py:473
  34.2 5.9 %shard_map.74 = f32[2,200,512]{2,1,0:T(8,128)} custom-call(s32[2]{0:T(128)S(1)} %pad_add_fusion.which.where_at, f32[4,2]{1,0:T(4,128)S(1)} %get-tuple-element.37.late_coeff, f32[4,2,256,256]{3,2,1,0:T(8,128)S(1)} %get-tuple-element.38.early, f32[8,256]{1,0:T(8,128)S(1)} %get-tuple-element.39.diags, f32[2,224,512]{2,1,0:T(8,128)S(1)} %get-tuple-element.40.source, ...), custom_call_target="tpu_custom_call" | custom-call | flops 10000000000 | bytes 10000000 | tf_op jit(solution)/shard_map/pallas_call | solution.py:489
  (29 shorter events, 0.7 us)
Async XLA Ops:
  0.6 7.7 %copy-start.2 = (f32[2,2]{1,0:T(2,128)S(1)}, f32[2,2]{1,0:T(2,128)}, u32[]{:S(2)}) copy-start(f32[2,2]{1,0:T(2,128)} %fields.1) | copy-start | bytes 52
  0.7 1.6 %copy-start = (f32[2,512,512]{2,1,0:T(8,128)S(1)}, f32[2,512,512]{2,1,0:T(8,128)}, u32[]{:S(2)}) copy-start(f32[2,512,512]{2,1,0:T(8,128)} %vec.1) | copy-start | bytes 6291460
  2.3 3.7 %copy-start.1 = (f32[2,512,200]{1,2,0:T(8,128)S(1)}, f32[2,512,200]{1,2,0:T(8,128)}, u32[]{:S(2)}) copy-start(f32[2,512,200]{1,2,0:T(8,128)} %param.5) | copy-start | bytes 2457604
  3.0 9.4 %collective-permute-start.8 = (f32[256,256]{1,0:T(8,128)S(1)}, f32[256,256]{1,0:T(8,128)S(1)}, u32[]{:S(2)}, u32[]{:S(2)}) collective-permute-start(f32[256,256]{1,0:T(8,128)S(1)} %get-tuple-element.31.refs_7_), channel_id=1, source_target_pairs={{0,1},{1,0},{2,3},{3,2},{4,5},{5,4},{6,7},{7,6},{8,9},{9,8},{10,11... | collective-permute-start | bytes 786440 | tf_op jit(solution)/shard_map/ppermute | solution.py:403
  6.0 11.6 %collective-permute-start.3 = (f32[2,200,512]{2,1,0:T(8,128)S(1)}, f32[2,200,512]{2,1,0:T(8,128)S(1)}, u32[]{:S(2)}, u32[]{:S(2)}) collective-permute-start(f32[2,200,512]{2,1,0:T(8,128)S(1)} %bitcast.4), channel_id=1, source_target_pairs={{4,8},{12,16},{20,24},{8,4},{16,12},{24,20},{0,0},{28,28},{5,9},{1... | collective-permute-start | bytes 2457608 | tf_op jit(solution)/shard_map/ppermute | solution.py:411
  6.7 8.3 %collective-permute-start.10 = (f32[256,256]{1,0:T(8,128)S(1)}, f32[256,256]{1,0:T(8,128)S(1)}, u32[]{:S(2)}, u32[]{:S(2)}) collective-permute-start(f32[256,256]{1,0:T(8,128)S(1)} %get-tuple-element.30.refs_8_), channel_id=1, source_target_pairs={{0,2},{1,3},{2,0},{3,1},{4,6},{5,7},{6,4},{7,5},{8,10},{9,11},{10,... | collective-permute-start | bytes 786440 | tf_op jit(solution)/shard_map/ppermute | solution.py:403
  8.3 8.6 %copy-start.3 = (f32[2]{0:T(128)S(1)}, f32[2]{0:T(128)}, u32[]{:S(2)}) copy-start(f32[2]{0:T(128)} %weights.1) | copy-start | bytes 28
  8.3 8.6 %copy-start.4 = (s32[2]{0:T(128)S(1)}, s32[2]{0:T(128)}, u32[]{:S(2)}) copy-start(s32[2]{0:T(128)} %counts.1) | copy-start | bytes 28
  11.4 4.1 %collective-permute-start = (f32[8,256]{1,0:T(8,128)S(1)}, f32[8,256]{1,0:T(8,128)S(1)}, u32[]{:S(2)}, u32[]{:S(2)}) collective-permute-start(f32[8,256]{1,0:T(8,128)S(1)} %shard_map.69.refs_0_.refs_3_), channel_id=1, source_target_pairs={{0,1},{1,0},{2,3},{3,2},{4,5},{5,4},{6,7},{7,6},{8,9},{9,8},{10,11... | collective-permute-start | bytes 24584 | tf_op jit(solution)/shard_map/ppermute | solution.py:403
  12.0 4.0 %collective-permute-start.1 = (f32[8,256]{1,0:T(8,128)S(1)}, f32[8,256]{1,0:T(8,128)S(1)}, u32[]{:S(2)}, u32[]{:S(2)}) collective-permute-start(f32[8,256]{1,0:T(8,128)S(1)} %shard_map.69.refs_0_.refs_3_), channel_id=1, source_target_pairs={{0,2},{1,3},{2,0},{3,1},{4,6},{5,7},{6,4},{7,5},{8,10},{9,11},{10,... | collective-permute-start | bytes 24584 | tf_op jit(solution)/shard_map/ppermute | solution.py:403
  12.4 4.6 %collective-permute-start.2 = (f32[8,256]{1,0:T(8,128)S(1)}, f32[8,256]{1,0:T(8,128)S(1)}, u32[]{:S(2)}, u32[]{:S(2)}) collective-permute-start(f32[8,256]{1,0:T(8,128)S(1)} %shard_map.69.refs_0_.refs_3_), channel_id=1, source_target_pairs={{0,3},{1,2},{2,1},{3,0},{4,7},{5,6},{6,5},{7,4},{8,11},{9,10},{10,... | collective-permute-start | bytes 24584 | tf_op jit(solution)/shard_map/ppermute | solution.py:403
  15.0 13.4 %collective-permute-start.9 = (f32[256,256]{1,0:T(8,128)S(1)}, f32[256,256]{1,0:T(8,128)S(1)}, u32[]{:S(2)}, u32[]{:S(2)}) collective-permute-start(f32[256,256]{1,0:T(8,128)S(1)} %get-tuple-element.30.refs_8_), channel_id=1, source_target_pairs={{0,1},{1,0},{2,3},{3,2},{4,5},{5,4},{6,7},{7,6},{8,9},{9,8},{10,11... | collective-permute-start | bytes 786440 | tf_op jit(solution)/shard_map/ppermute | solution.py:403
  15.6 12.9 %collective-permute-start.11 = (f32[256,256]{1,0:T(8,128)S(1)}, f32[256,256]{1,0:T(8,128)S(1)}, u32[]{:S(2)}, u32[]{:S(2)}) collective-permute-start(f32[256,256]{1,0:T(8,128)S(1)} %get-tuple-element.31.refs_7_), channel_id=1, source_target_pairs={{0,2},{1,3},{2,0},{3,1},{4,6},{5,7},{6,4},{7,5},{8,10},{9,11},{10,... | collective-permute-start | bytes 786440 | tf_op jit(solution)/shard_map/ppermute | solution.py:403
  17.6 4.4 %collective-permute-start.4 = (f32[1,256]{1,0:T(1,128)S(1)}, f32[1,256]{1,0:T(1,128)S(1)}, u32[]{:S(2)}, u32[]{:S(2)}) collective-permute-start(f32[1,256]{1,0:T(1,128)S(1)} %shard_map.70), channel_id=1, source_target_pairs={{0,4},{4,0},{8,12},{12,8},{16,20},{20,16},{24,28},{28,24},{1,5},{5... | collective-permute-start | bytes 3080 | tf_op jit(solution)/shard_map/ppermute | solution.py:464
  19.9 10.3 %collective-permute-start.13 = (f32[256,256]{1,0:T(8,128)S(1)}, f32[256,256]{1,0:T(8,128)S(1)}, u32[]{:S(2)}, u32[]{:S(2)}) collective-permute-start(f32[256,256]{1,0:T(8,128)S(1)} %collective-permute-done.8.refs_0_.refs_9_), channel_id=1, source_target_pairs={{0,2},{1,3},{2,0},{3,1},{4,6},{5,7},{6,4},{7,5},{8,10},{9,11},{10,... | collective-permute-start | bytes 786440 | tf_op jit(solution)/shard_map/ppermute | solution.py:403
  21.4 8.8 %collective-permute-start.14 = (f32[256,256]{1,0:T(8,128)S(1)}, f32[256,256]{1,0:T(8,128)S(1)}, u32[]{:S(2)}, u32[]{:S(2)}) collective-permute-start(f32[256,256]{1,0:T(8,128)S(1)} %collective-permute-done.10.refs_3_.refs_12_), channel_id=1, source_target_pairs={{0,1},{1,0},{2,3},{3,2},{4,5},{5,4},{6,7},{7,6},{8,9},{9,8},{10,11... | collective-permute-start | bytes 786440 | tf_op jit(solution)/shard_map/ppermute | solution.py:403
  22.0 3.7 %collective-permute-start.5 = (f32[2,256]{1,0:T(2,128)S(1)}, f32[2,256]{1,0:T(2,128)S(1)}, u32[]{:S(2)}, u32[]{:S(2)}) collective-permute-start(f32[2,256]{1,0:T(2,128)S(1)} %pad_maximum_fusion.2), channel_id=1, source_target_pairs={{0,8},{4,12},{8,0},{12,4},{16,24},{20,28},{24,16},{28,20},{1,9},{5... | collective-permute-start | bytes 6152 | tf_op jit(solution)/shard_map/ppermute | solution.py:464
  25.7 4.6 %collective-permute-start.6 = (f32[4,256]{1,0:T(4,128)S(1)}, f32[4,256]{1,0:T(4,128)S(1)}, u32[]{:S(2)}, u32[]{:S(2)}) collective-permute-start(f32[4,256]{1,0:T(4,128)S(1)} %pad_maximum_fusion.1), channel_id=1, source_target_pairs={{0,16},{4,20},{8,24},{12,28},{16,0},{20,4},{24,8},{28,12},{1,17},{... | collective-permute-start | bytes 12296 | tf_op jit(solution)/shard_map/ppermute | solution.py:464
  28.5 2.3 %collective-permute-start.7 = (f32[2,200,512]{2,1,0:T(8,128)S(1)}, f32[2,200,512]{2,1,0:T(8,128)S(1)}, u32[]{:S(2)}, u32[]{:S(2)}) collective-permute-start(f32[2,200,512]{2,1,0:T(8,128)S(1)} %bitcast.6), channel_id=1, source_target_pairs={{0,4},{4,0},{8,12},{12,8},{16,20},{20,16},{24,28},{28,24},{1,5},{5... | collective-permute-start | bytes 2457608 | tf_op jit(solution)/shard_map/ppermute | solution.py:406
  28.5 3.7 %collective-permute-start.12 = (f32[1024,256]{1,0:T(8,128)S(1)}, f32[1024,256]{1,0:T(8,128)S(1)}, u32[]{:S(2)}, u32[]{:S(2)}) collective-permute-start(f32[1024,256]{1,0:T(8,128)S(1)} %shard_map.71), channel_id=1, source_target_pairs={{0,4},{4,0},{8,12},{12,8},{16,20},{20,16},{24,28},{28,24},{1,5},{5... | collective-permute-start | bytes 3145736 | tf_op jit(solution)/shard_map/ppermute | solution.py:406
  30.3 3.9 %collective-permute-start.15 = (f32[512,256]{1,0:T(8,128)S(1)}, f32[512,256]{1,0:T(8,128)S(1)}, u32[]{:S(2)}, u32[]{:S(2)}) collective-permute-start(f32[512,256]{1,0:T(8,128)S(1)} %shard_map.73), channel_id=1, source_target_pairs={{0,4},{4,0},{8,12},{12,8},{16,20},{20,16},{24,28},{28,24},{1,5},{5... | collective-permute-start | bytes 1572872 | tf_op jit(solution)/shard_map/ppermute | solution.py:406
